TPU v7x, 32 devices: a whole 2x2x4 slice. The times are simulated.
32 devices in a mesh: row: 4 (over z), col: 8 (over y, x, core).
Axes of the slice: x: 2, y: 2, z: 4, core: 2. Of those that a mesh axis runs over, the one named last changes fastest.
Arguments:
- tokens: bfloat16 [128, 128, 512], P('row', 'col'), may hold values from -6 to 6
- norm_gains: float32 [4, 512], replicated, may hold values from 0.1 to 1.9
- qkv_weight: bfloat16 [2, 512, 1536], replicated, may hold values from -1 to 1
- rel_bias: float32 [2, 16, 13, 13], replicated, may hold values from -4 to 4
- proj_weight: bfloat16 [2, 512, 512], replicated, may hold values from -0.5 to 0.5
- up_weight: bfloat16 [2, 512, 2048], replicated, may hold values from -0.25 to 0.25
- down_weight: bfloat16 [2, 2048, 512], replicated, may hold values from -0.125 to 0.125
Outputs:
- features: bfloat16 [128, 128, 512], P('row', 'col')
All inputs are finite; a program needn't handle non-finite values.
Results may differ from a plain program's by a relative error of at most 0.014.
Values may be sent and summed in bfloat16 or wider, within the bound.
A program may use at most 320 MiB of HBM per device.

v0:
```python
import jax
import jax.numpy as jnp
from jax import lax
from jax.sharding import PartitionSpec as P

DILATION = 16


def padded_2(cells, sides, width):
    for axis, dim in sides:
        count = lax.axis_size(axis)
        ends = count - 1
        head = lax.slice_in_dim(cells, 0, width, axis=dim)
        tail = lax.slice_in_dim(cells, cells.shape[dim] - width, cells.shape[dim], axis=dim)
        cells = jnp.concatenate(
            [
                lax.ppermute(tail, axis, [(i, (i + 1) % count) for i in range(ends)]),
                cells,
                lax.ppermute(head, axis, [((i + 1) % count, i) for i in range(ends)]),
            ],
            axis=dim,
        )
    return cells


def window_starts(positions, extent):
    return jnp.clip(positions - 3, 0, extent - 7)


def layer_norm(rows_in, norm_gain):
    values_f = rows_in.astype(jnp.float32)
    mean_value = jnp.mean(values_f, axis=-1, keepdims=True)
    centred = values_f - mean_value
    variance = jnp.mean(centred * centred, axis=-1, keepdims=True)
    return (centred * lax.rsqrt(variance + 1e-05) * norm_gain).astype(jnp.bfloat16)


def window_attend(
    queries, key_block, value_block, row_start, col_start, row_shift, col_shift, rel_table
):
    query_rows, query_cols, group_count, feature_width = queries.shape
    head_count = rel_table.shape[0]
    head_size = feature_width // head_count
    token_count = query_rows * query_cols * group_count
    query_flat = queries.reshape(token_count, feature_width)
    head_ones = (
        jnp.arange(feature_width, dtype=jnp.int32)[None, :] // head_size
        == jnp.arange(head_count, dtype=jnp.int32)[:, None]
    ).astype(jnp.float32)
    head_mask = head_ones.astype(jnp.bfloat16)
    classes = jnp.arange(13, dtype=jnp.int32)
    col_hots = [
        ((col_shift + across + 6)[:, None] == classes).astype(jnp.float32) for across in range(7)
    ]
    scaling = head_size ** (-0.5)
    score_list = []
    for offset in range(7):
        key_rows = jnp.take(key_block, row_start + offset, axis=0)
        row_hot = ((row_shift + offset + 6)[:, None] == classes).astype(jnp.float32)
        for across in range(7):
            window = jnp.take(key_rows, col_start + across, axis=1).reshape(
                token_count, feature_width
            )
            product = query_flat.astype(jnp.float32) * window.astype(jnp.float32)
            partial_score = jnp.einsum(
                "nd,td->nt", head_ones, product, precision=lax.Precision.HIGHEST
            )
            bias_term = jnp.einsum(
                "iy,cz,nyz->nic",
                row_hot,
                col_hots[across],
                rel_table,
                precision=lax.Precision.HIGHEST,
            )
            bias_full = jnp.broadcast_to(
                bias_term[:, :, :, None], (head_count, query_rows, query_cols, group_count)
            ).reshape(head_count, token_count)
            score_list.append(partial_score * scaling + bias_full)
    scores = jnp.stack(score_list)
    row_max = jnp.max(scores, axis=0, keepdims=True)
    exponent = jnp.exp(scores - row_max)
    weights = (exponent / jnp.sum(exponent, axis=0, keepdims=True)).astype(jnp.bfloat16)
    running = jnp.zeros((token_count, feature_width), jnp.float32)
    for offset in range(7):
        value_rows = jnp.take(value_block, row_start + offset, axis=0)
        for across in range(7):
            window = jnp.take(value_rows, col_start + across, axis=1).reshape(
                token_count, feature_width
            )
            spread = jnp.einsum(
                "nt,nd->td",
                weights[offset * 7 + across],
                head_mask,
                preferred_element_type=jnp.float32,
            )
            running = running + spread * window.astype(jnp.float32)
    return running.reshape(query_rows, query_cols, group_count, feature_width).astype(jnp.bfloat16)


def finish_layer(attended, stream, norm_gain, proj, up_proj, down_proj):
    mixed = (
        jnp.dot(attended, proj, preferred_element_type=jnp.float32) + stream.astype(jnp.float32)
    ).astype(jnp.bfloat16)
    normed = layer_norm(mixed, norm_gain)
    hidden = jax.nn.gelu(
        jnp.dot(normed, up_proj, preferred_element_type=jnp.float32), approximate=True
    ).astype(jnp.bfloat16)
    return (
        jnp.dot(hidden, down_proj, preferred_element_type=jnp.float32) + mixed.astype(jnp.float32)
    ).astype(jnp.bfloat16)


def body(tokens, norm_gains, qkv_weight, rel_bias, proj_weight, up_weight, down_weight):
    tile_rows, tile_cols, feature_width = tokens.shape
    row_count = lax.axis_size("row")
    col_count = lax.axis_size("col")
    map_rows = tile_rows * row_count
    map_cols = tile_cols * col_count
    stream_rows = tokens.reshape(-1, feature_width)
    normed = layer_norm(stream_rows, norm_gains[0])
    rim_inputs = padded_2(
        normed.reshape(tile_rows, tile_cols, feature_width), (("row", 0), ("col", 1)), 3
    )
    queries = jnp.dot(
        normed, qkv_weight[0][:, :feature_width], preferred_element_type=jnp.float32
    ).astype(jnp.bfloat16)
    padded = jnp.dot(
        rim_inputs.reshape(-1, feature_width),
        qkv_weight[0][:, feature_width:],
        preferred_element_type=jnp.float32,
    ).astype(jnp.bfloat16)
    padded = padded.reshape(tile_rows + 6, tile_cols + 6, 2 * feature_width)
    key_block = padded[:, :, None, :feature_width]
    value_block = padded[:, :, None, feature_width:]
    first_row = lax.axis_index("row") * tile_rows
    first_col = lax.axis_index("col") * tile_cols
    row_global = first_row + jnp.arange(tile_rows, dtype=jnp.int32)
    col_global = first_col + jnp.arange(tile_cols, dtype=jnp.int32)
    row_begin = window_starts(row_global, map_rows)
    col_begin = window_starts(col_global, map_cols)
    attended = window_attend(
        queries.reshape(tile_rows, tile_cols, 1, feature_width),
        key_block,
        value_block,
        row_begin - first_row + 3,
        col_begin - first_col + 3,
        row_begin - row_global,
        col_begin - col_global,
        rel_bias[0],
    )
    stream_rows = finish_layer(
        attended.reshape(-1, feature_width),
        stream_rows,
        norm_gains[1],
        proj_weight[0],
        up_weight[0],
        down_weight[0],
    )
    residue_rows = DILATION // row_count
    residue_cols = DILATION // col_count
    block_rows = tile_rows // DILATION
    block_cols = tile_cols // DILATION
    group_rows = block_rows * row_count
    group_cols = block_cols * col_count
    group_count = residue_rows * residue_cols
    shaped = stream_rows.reshape(
        block_rows, row_count, residue_rows, block_cols, col_count, residue_cols, feature_width
    )
    shaped = shaped.transpose(1, 4, 2, 5, 0, 3, 6).reshape(
        row_count * col_count, residue_rows, residue_cols, block_rows * block_cols, feature_width
    )
    arrived = lax.all_to_all(shaped, ("row", "col"), split_axis=0, concat_axis=0, tiled=True)
    grouped = arrived.reshape(
        row_count, col_count, residue_rows, residue_cols, block_rows, block_cols, feature_width
    )
    grouped = grouped.transpose(0, 4, 1, 5, 2, 3, 6).reshape(
        group_rows, group_cols, group_count, feature_width
    )
    grouped_rows = grouped.reshape(-1, feature_width)
    packed_two = jnp.dot(
        layer_norm(grouped_rows, norm_gains[2]), qkv_weight[1], preferred_element_type=jnp.float32
    ).astype(jnp.bfloat16)
    packed_two = packed_two.reshape(group_rows, group_cols, group_count, 3 * feature_width)
    bordered = jnp.pad(packed_two[..., feature_width:], ((3, 3), (3, 3), (0, 0), (0, 0)))
    grow_places = jnp.arange(group_rows, dtype=jnp.int32)
    gcol_places = jnp.arange(group_cols, dtype=jnp.int32)
    grow_begin = window_starts(grow_places, group_rows)
    gcol_begin = window_starts(gcol_places, group_cols)
    attended_two = window_attend(
        packed_two[..., :feature_width],
        bordered[..., :feature_width],
        bordered[..., feature_width:],
        grow_begin + 3,
        gcol_begin + 3,
        grow_begin - grow_places,
        gcol_begin - gcol_places,
        rel_bias[1],
    )
    final_rows = finish_layer(
        attended_two.reshape(-1, feature_width),
        grouped_rows,
        norm_gains[3],
        proj_weight[1],
        up_weight[1],
        down_weight[1],
    )
    shaped = final_rows.reshape(
        row_count, block_rows, col_count, block_cols, residue_rows, residue_cols, feature_width
    )
    shaped = shaped.transpose(0, 2, 4, 5, 1, 3, 6).reshape(
        row_count * col_count, residue_rows, residue_cols, block_rows * block_cols, feature_width
    )
    arrived = lax.all_to_all(shaped, ("row", "col"), split_axis=0, concat_axis=0, tiled=True)
    restored = arrived.reshape(
        row_count, col_count, residue_rows, residue_cols, block_rows, block_cols, feature_width
    )
    restored = restored.transpose(4, 0, 2, 5, 1, 3, 6).reshape(tile_rows, tile_cols, feature_width)
    return restored


def solution(mesh):
    placed = (P("row", "col", None), P(), P(), P(), P(), P(), P())
    return jax.shard_map(
        body, mesh=mesh, in_specs=placed, out_specs=P("row", "col", None), check_vma=False
    )
```

profile of v0, /device:TPU:0, one launch (start us, length us, event | category | flops | bytes accessed | tf_op | source)
XLA Modules:
  0.0 1171.1 jit_solution(8854914096301710201)
XLA Ops:
  7.5 6.2 collective-permute-start
  139.5 3.7 collective-permute-start.2
  215.3 2.8 fusion.267
  454.3 5.7 fusion.288
  463.4 6.7 fusion.287
  471.8 7.9 fusion.286
  479.7 2.9 copy.1463
  482.6 8.3 fusion.285
  490.9 2.9 copy.1467
  493.8 8.3 fusion.284
  502.1 2.9 copy.1471
  504.9 8.3 fusion.283
  513.2 2.9 copy.1475
  516.1 8.2 fusion.282
  524.3 3.0 copy.1479
  659.8 5.6 fusion.140
  667.0 5.3 all-to-all-start
  739.9 2.6 broadcast_select_fusion.8
  747.7 2.9 broadcast_select_fusion.6
  755.7 2.9 broadcast_select_fusion.4
  763.8 2.9 broadcast_select_fusion.2
  771.8 2.9 broadcast_select_fusion.13
  800.4 2.6 gather_fusion.125
  813.2 2.6 gather_fusion.117
  833.7 2.7 gather_fusion.167
  957.7 2.6 gather_fusion.175
  970.3 4.3 bitcast_convert_fusion.6
  979.8 7.6 convert_multiply_fusion.4
  990.9 8.8 convert_multiply_fusion.2
  1003.3 9.0 convert_multiply_fusion
  1141.4 5.4 fusion.143
  1147.7 21.2 %all_to_all.10 = bf16[32,4,2,2,512]{4,3,2,1,0:T(2,128)(2,1)S(1)} all-to-all(bf16[32,4,2,2,512]{4,3,2,1,0:T(2,128)(2,1)S(1)} %copy.1952), channel_id=1, replica_groups=mesh['row'=4,'col'=8] {'row','col'}, dimensions={0} | all-to-all | bytes 1048576 | tf_op jit(solution)/shard_map/all_to_all | solution.py:213
  (2051 shorter events, 990.9 us)
Async XLA Ops:
  0.0 13.7 %copy-start.17 = (bf16[32,16,512]{2,1,0:T(8,128)(2,1)S(1)}, bf16[32,16,512]{2,1,0:T(8,128)(2,1)}, u32[]{:S(2)}) copy-start(bf16[32,16,512]{2,1,0:T(8,128)(2,1)} %param.15) | copy-start | bytes 1572868
  1.3 23.4 %copy-start.297 = (f32[2,16,13,13]{1,0,3,2:T(2,128)S(1)}, f32[2,16,13,13]{1,0,3,2:T(2,128)}, u32[]{:S(2)}) copy-start(f32[2,16,13,13]{1,0,3,2:T(2,128)} %param.18) | copy-start | bytes 64900
  6.2 130.2 %collective-permute-start.1 = (bf16[3,16,512]{2,1,0:T(8,128)(2,1)}, bf16[3,16,512]{2,1,0:T(8,128)(2,1)}, u32[]{:S(2)}, u32[]{:S(2)}) collective-permute-start(bf16[3,16,512]{2,1,0:T(8,128)(2,1)} %bitcast.4), channel_id=1, source_target_pairs={{8,0},{16,8},{24,16},{9,1},{17,9},{25,17},{10,2},{18,10},{26,18},{... | collective-permute-start | bytes 147464 | tf_op jit(solution)/shard_map/ppermute | solution.py:19
  7.5 129.0 %collective-permute-start = (bf16[3,16,512]{2,1,0:T(8,128)(2,1)}, bf16[3,16,512]{2,1,0:T(8,128)(2,1)}, u32[]{:S(2)}, u32[]{:S(2)}) collective-permute-start(bf16[3,16,512]{2,1,0:T(8,128)(2,1)} %bitcast.3), channel_id=1, source_target_pairs={{0,8},{8,16},{16,24},{1,9},{9,17},{17,25},{2,10},{10,18},{18,26},{... | collective-permute-start | bytes 147464 | tf_op jit(solution)/shard_map/ppermute | solution.py:17
  121.9 8.2 copy-start.292
  126.5 6.3 copy-start.293
  126.5 7.2 copy-start.294
  132.9 10.3 copy-start.283
  133.8 10.3 copy-start.281
  134.8 10.3 copy-start.284
  135.7 10.3 copy-start.286
  138.1 8.7 copy-start.288
  138.1 47.9 %collective-permute-start.3 = (bf16[38,3,512]{2,1,0:T(4,128)(2,1)}, bf16[38,3,512]{2,1,0:T(4,128)(2,1)}, u32[]{:S(2)}, u32[]{:S(2)}) collective-permute-start(bf16[38,3,512]{2,1,0:T(4,128)(2,1)} %get-tuple-element.14), channel_id=1, source_target_pairs={{1,0},{2,1},{3,2},{4,3},{5,4},{6,5},{7,6},{9,8},{10,9},{11,10},{12... | collective-permute-start | bytes 350216 | tf_op jit(solution)/shard_map/ppermute | solution.py:19
  139.5 46.5 %collective-permute-start.2 = (bf16[38,3,512]{2,1,0:T(4,128)(2,1)}, bf16[38,3,512]{2,1,0:T(4,128)(2,1)}, u32[]{:S(2)}, u32[]{:S(2)}) collective-permute-start(bf16[38,3,512]{2,1,0:T(4,128)(2,1)} %get-tuple-element.13), channel_id=1, source_target_pairs={{0,1},{1,2},{2,3},{3,4},{4,5},{5,6},{6,7},{8,9},{9,10},{10,11},{11... | collective-permute-start | bytes 350216 | tf_op jit(solution)/shard_map/ppermute | solution.py:17
  146.9 6.2 copy-start.290
  147.9 6.2 copy-start.287
  148.8 6.2 copy-start.285
  186.0 263.8 %copy-start.441 = (s32[1024]{0:T(1024)}, s32[1024]{0:T(1024)S(1)}, u32[]{:S(2)}) copy-start(s32[1024]{0:T(1024)S(1)} %get-tuple-element.495) | copy-start | bytes 12292
  238.5 6.0 copy-start.479
  253.1 7.3 copy-start.480
  305.1 7.2 copy-start.438
  665.6 6.7 copy-start.346
  665.7 7.4 copy-start.345
  665.7 8.2 copy-start.344
  667.0 7.6 copy-start.343
  667.0 8.3 copy-start.342
  667.0 35.9 %all-to-all-start = ((bf16[32,4,2,2,512]{4,3,2,1,0:T(2,128)(2,1)}), bf16[32,4,2,2,512]{4,3,2,1,0:T(2,128)(2,1)S(1)}, u32[]{:S(2)}, u32[]{:S(2)}) async-start(bf16[32,4,2,2,512]{4,3,2,1,0:T(2,128)(2,1)} %copy.1749), calls=%async_computation | async-start | bytes 1048576 | tf_op jit(solution)/shard_map/all_to_all | solution.py:172
  702.8 61.0 %copy-start.444 = (pred[8]{0:T(512)(128)(4,1)}, pred[8]{0:T(512)(128)(4,1)S(1)}, u32[]{:S(2)}) copy-start(pred[8]{0:T(512)(128)(4,1)S(1)} %get-tuple-element.519) | copy-start | bytes 28
  702.8 32.6 %copy-start.452 = (pred[8]{0:T(512)(128)(4,1)}, pred[8]{0:T(512)(128)(4,1)S(1)}, u32[]{:S(2)}) copy-start(pred[8]{0:T(512)(128)(4,1)S(1)} %get-tuple-element.515) | copy-start | bytes 28
  702.9 37.1 %copy-start.450 = (pred[8]{0:T(512)(128)(4,1)}, pred[8]{0:T(512)(128)(4,1)S(1)}, u32[]{:S(2)}) copy-start(pred[8]{0:T(512)(128)(4,1)S(1)} %get-tuple-element.514) | copy-start | bytes 28
  702.9 44.8 %copy-start.448 = (pred[8]{0:T(512)(128)(4,1)}, pred[8]{0:T(512)(128)(4,1)S(1)}, u32[]{:S(2)}) copy-start(pred[8]{0:T(512)(128)(4,1)S(1)} %get-tuple-element.517) | copy-start | bytes 28
  702.9 52.8 %copy-start.446 = (pred[8]{0:T(512)(128)(4,1)}, pred[8]{0:T(512)(128)(4,1)S(1)}, u32[]{:S(2)}) copy-start(pred[8]{0:T(512)(128)(4,1)S(1)} %get-tuple-element.516) | copy-start | bytes 28
  (459 other events, 1058.0 us)
where the time goes:
time: 1190 us; the launch traced here: 1170 us
  local copies, waits for them, and re-layouts  754 us (63%)
  matrix products  206 us (17%)
  other arithmetic  165 us (14%)
  blocking collectives  21.2 us (2%)
  starting transfers between devices  17.8 us (1%)
    gather x98, local copies, waits for them, and re-layouts, window_attend(): jnp.take(key_rows, col_start + across, axis=1)  216 us
    gather x98, local copies, waits for them, and re-layouts, window_attend(): jnp.take(value_rows, col_start + across, axis=1)  206 us
    dot_general x112, matrix products, window_attend(): jnp.einsum('iy,cz,nyz->nic', row_hot, col_hots[across], rel_table, precis...  89.5 us
    convert_element_type x14, other arithmetic, window_attend(): running = running + spread * window.astype(jnp.float32)  70 us
    dot_general x98, matrix products, window_attend(): jnp.einsum('nd,td->nt', head_ones, product, precision=lax.Precision.HIGHEST)  61.4 us
    unnamed x974, local copies, waits for them, and re-layouts  53.9 us
    convert_element_type x49, local copies, waits for them, and re-layouts, window_attend(): product = query_flat.astype(jnp.float32) * window.astype(jnp.float32)  53.2 us
    convert_element_type x98, local copies, waits for them, and re-layouts, window_attend(): running = running + spread * window.astype(jnp.float32)  45.2 us
  transfers between devices with their start and end apart: 5, of which 0 were waited for; matrix products, arithmetic and copies ran while one was open for 17% of the time, Pallas kernels for 0%

commit v1 on v0

v1 whole, which is shorter than its diff:
```python
import functools
import math

import jax
import jax.numpy as jnp
from jax import lax
from jax.experimental import pallas as pl
from jax.experimental.pallas import tpu as pltpu
from jax.sharding import PartitionSpec as P

DILATION = 16
REACH = 6
HALO = 4
QUERY_ROWS = 8
MASKED = -1e30
LOG2E = 1.4426950408889634
VMEM_BYTES = 56 * 1024 * 1024


def layer_norm(values, gain):
    values_f = values.astype(jnp.float32)
    mean_value = jnp.mean(values_f, axis=-1, keepdims=True)
    centred = values_f - mean_value
    variance = jnp.mean(centred * centred, axis=-1, keepdims=True)
    return (centred * lax.rsqrt(variance + 1e-05) * gain).astype(jnp.bfloat16)


def dot(left, right):
    return jnp.dot(left, right, preferred_element_type=jnp.float32)


def bias_rows(rel, q_rows, k_rows, q_cols, k_cols, row_off, col_off):
    heads, classes, _ = rel.shape
    extent = q_rows + k_rows - 1
    before = q_rows - 1 + row_off - REACH
    left = q_cols + col_off
    padded = jnp.pad(
        rel * LOG2E,
        ((0, 0), (before, extent - before - classes), (left, k_cols + q_cols)),
    )
    starts = [left + REACH - col_off - place for place in range(q_cols)]
    rows = [padded[:, :, start : start + k_cols] for start in starts]
    return jnp.stack(rows, axis=1).reshape(heads, q_cols, extent * k_cols)


def in_window(query, key, extent):
    start = jnp.clip(query - 3, 0, extent - 7)
    return (key >= start) & (key < start + 7)


def head_lanes(lanes, head_size):
    lane = lax.broadcasted_iota(jnp.int32, (1, lanes), 1)
    return [(lane // head_size) == h for h in range(lanes // head_size)]


def attend(queries, keys, values, bias, mask, head_size):
    count, lanes = queries.shape
    picks = head_lanes(lanes, head_size)
    zero = jnp.zeros_like(queries)
    stacked = jnp.concatenate([jnp.where(pick, queries, zero) for pick in picks], axis=0)
    scores = lax.dot_general(
        stacked, keys, (((1,), (1,)), ((), ())), preferred_element_type=jnp.float32
    )
    scores = scores.reshape(len(picks), count, keys.shape[0]) + bias
    if mask is not None:
        scores = scores + mask[None]
    peak = jnp.max(scores, axis=-1, keepdims=True)
    weights = jnp.exp2(scores - peak).astype(jnp.bfloat16)
    wide = jnp.concatenate([values, jnp.ones_like(values)], axis=1)
    summed = dot(weights.reshape(len(picks) * count, keys.shape[0]), wide)
    ratio = summed[:, :lanes] / summed[:, lanes:]
    result = ratio[:count]
    for h in range(1, len(picks)):
        result = jnp.where(picks[h], ratio[h * count : (h + 1) * count], result)
    return result.astype(jnp.bfloat16)


def finish(att_ref, x_ref, gain, proj_ref, up_ref, down_ref, out_ref, chunk):
    width = x_ref.shape[1]
    hidden_width = up_ref.shape[1]
    part = math.gcd(hidden_width, 512)

    def step(index, carry):
        rows = pl.ds(pl.multiple_of(index * chunk, chunk), chunk)
        mixed = (dot(att_ref[rows, :], proj_ref[...]) + x_ref[rows, :].astype(jnp.float32)).astype(
            jnp.bfloat16
        )
        normed = layer_norm(mixed, gain)
        total = mixed.astype(jnp.float32)
        for first in range(0, hidden_width, part):
            hidden = jax.nn.gelu(dot(normed, up_ref[:, first : first + part]), approximate=True)
            total = total + dot(hidden.astype(jnp.bfloat16), down_ref[first : first + part, :])
        out_ref[rows, :] = total.astype(jnp.bfloat16)
        return carry

    lax.fori_loop(0, x_ref.shape[0] // chunk, step, 0)


def project(src_ref, gain, weight, dst_ref, scale, chunk):
    def step(index, carry):
        rows = pl.ds(pl.multiple_of(index * chunk, chunk), chunk)
        result = dot(layer_norm(src_ref[rows, :], gain), weight)
        if scale is not None:
            result = result * scale
        dst_ref[rows, :] = result.astype(jnp.bfloat16)
        return carry

    lax.fori_loop(0, src_ref.shape[0] // chunk, step, 0)


def local_kernel(
    geometry, x_ref, pad_ref, gains_ref, qkv_ref, bias_ref, proj_ref, up_ref, down_ref, out_ref,
    q_ref, kv_ref, full_ref, att_ref,
):
    tile_rows, tile_cols, map_rows, map_cols, heads = geometry
    width = x_ref.shape[1]
    head_size = width // heads
    lanes = 128
    per = lanes // head_size
    wide_cols = tile_cols + 2 * HALO
    key_rows = QUERY_ROWS + 2 * HALO
    n_query = QUERY_ROWS * tile_cols
    n_key = key_rows * wide_cols
    scale = head_size ** (-0.5) * LOG2E
    gain = gains_ref[0:1, :]
    for n in range(heads):
        for i in range(QUERY_ROWS):
            start = (QUERY_ROWS - 1 - i) * wide_cols
            full_ref[n, i * tile_cols : (i + 1) * tile_cols, :] = bias_ref[n, :, start : start + n_key]
    project(x_ref, gain, qkv_ref[:, :width], q_ref, scale, 256)
    project(pad_ref, gain, qkv_ref[:, width:], kv_ref, None, math.gcd(pad_ref.shape[0], 320))
    first_row = lax.axis_index("row") * tile_rows
    first_col = lax.axis_index("col") * tile_cols
    query = lax.broadcasted_iota(jnp.int32, (n_query, 1), 0)
    key = lax.broadcasted_iota(jnp.int32, (1, n_key), 1)
    query_row = query // tile_cols
    query_col = first_col + query - query_row * tile_cols
    key_row = key // wide_cols
    key_col = first_col + key - key_row * wide_cols - HALO
    col_seen = in_window(query_col, key_col, map_cols)

    def step(block, carry):
        top = first_row + block * QUERY_ROWS
        seen = col_seen & in_window(top + query_row, top + key_row - HALO, map_rows)
        mask = jnp.where(seen, 0.0, MASKED).astype(jnp.float32)
        q_rows = pl.ds(pl.multiple_of(block * n_query, n_query), n_query)
        k_first = QUERY_ROWS * wide_cols
        k_rows = pl.ds(pl.multiple_of(block * k_first, k_first), n_key)
        for g in range(width // lanes):
            cols = slice(g * lanes, (g + 1) * lanes)
            v_cols = slice(width + g * lanes, width + (g + 1) * lanes)
            att_ref[q_rows, cols] = attend(
                q_ref[q_rows, cols],
                kv_ref[k_rows, cols],
                kv_ref[k_rows, v_cols],
                full_ref[g * per : (g + 1) * per],
                mask,
                head_size,
            )
        return carry

    lax.fori_loop(0, tile_rows // QUERY_ROWS, step, 0)
    finish(att_ref, x_ref, gains_ref[1:2, :], proj_ref, up_ref, down_ref, out_ref, 256)


def group_kernel(
    geometry, x_ref, gains_ref, qkv_ref, bias_ref, proj_ref, up_ref, down_ref, out_ref,
    q_ref, kv_ref, full_ref, att_ref,
):
    group_rows, group_cols, heads, pack = geometry
    width = x_ref.shape[1]
    head_size = width // heads
    lanes = 128
    per = lanes // head_size
    size = group_rows * group_cols
    n_query = pack * size
    scale = head_size ** (-0.5) * LOG2E
    gain = gains_ref[2:3, :]
    query = lax.broadcasted_iota(jnp.int32, (n_query, 1), 0)
    key = lax.broadcasted_iota(jnp.int32, (1, n_query), 1)
    query_row, key_row = query // group_cols, key // group_cols
    query_col, key_col = query - query_row * group_cols, key - key_row * group_cols
    query_group, key_group = query // size, key // size
    seen = (
        (query_group == key_group)
        & in_window(query_row - query_group * group_rows, key_row - key_group * group_rows, group_rows)
        & in_window(query_col, key_col, group_cols)
    )
    for n in range(heads):
        for i in range(group_rows):
            start = (group_rows - 1 - i) * group_cols
            strip = bias_ref[n, :, start : start + size]
            strip = jnp.concatenate([strip] * pack, axis=1)
            for t in range(pack):
                first = t * size + i * group_cols
                full_ref[n, first : first + group_cols, :] = strip
        full_ref[n] = jnp.where(seen, full_ref[n], MASKED)
    project(x_ref, gain, qkv_ref[:, :width], q_ref, scale, 256)
    project(x_ref, gain, qkv_ref[:, width:], kv_ref, None, 256)

    def step(block, carry):
        rows = pl.ds(pl.multiple_of(block * n_query, n_query), n_query)
        for g in range(width // lanes):
            cols = slice(g * lanes, (g + 1) * lanes)
            v_cols = slice(width + g * lanes, width + (g + 1) * lanes)
            att_ref[rows, cols] = attend(
                q_ref[rows, cols],
                kv_ref[rows, cols],
                kv_ref[rows, v_cols],
                full_ref[g * per : (g + 1) * per],
                None,
                head_size,
            )
        return carry

    lax.fori_loop(0, x_ref.shape[0] // n_query, step, 0)
    finish(att_ref, x_ref, gains_ref[3:4, :], proj_ref, up_ref, down_ref, out_ref, 256)


def whole(array):
    return pl.BlockSpec(array.shape, lambda i: (0,) * array.ndim)


def one_layer(array, layer):
    return pl.BlockSpec((None,) + array.shape[1:], lambda i: (layer,) + (0,) * (array.ndim - 1))


def call_layer(kernel, layer, acts, gains, bias, weights, key_count, n_query, n_key):
    qkv, proj, up, down = weights
    rows, width = acts[0].shape
    heads = bias.shape[0]
    return pl.pallas_call(
        kernel,
        grid=(1,),
        out_shape=jax.ShapeDtypeStruct((rows, width), jnp.bfloat16),
        in_specs=[whole(act) for act in acts]
        + [whole(gains), one_layer(qkv, layer), whole(bias)]
        + [one_layer(weight, layer) for weight in (proj, up, down)],
        out_specs=pl.BlockSpec((rows, width), lambda i: (0, 0)),
        scratch_shapes=[
            pltpu.VMEM((rows, width), jnp.bfloat16),
            pltpu.VMEM((key_count, 2 * width), jnp.bfloat16),
            pltpu.VMEM((heads, n_query, n_key), jnp.float32),
            pltpu.VMEM((rows, width), jnp.bfloat16),
        ],
        compiler_params=pltpu.CompilerParams(vmem_limit_bytes=VMEM_BYTES),
    )(*acts, gains, qkv, bias, proj, up, down)


def padded(cells, axis, dim, width):
    count = lax.axis_size(axis)
    head = lax.slice_in_dim(cells, 0, width, axis=dim)
    tail = lax.slice_in_dim(cells, cells.shape[dim] - width, cells.shape[dim], axis=dim)
    return jnp.concatenate(
        [
            lax.ppermute(tail, axis, [(i, i + 1) for i in range(count - 1)]),
            cells,
            lax.ppermute(head, axis, [(i + 1, i) for i in range(count - 1)]),
        ],
        axis=dim,
    )


def body(tokens, norm_gains, qkv_weight, rel_bias, proj_weight, up_weight, down_weight):
    tile_rows, tile_cols, width = tokens.shape
    row_count = lax.axis_size("row")
    col_count = lax.axis_size("col")
    map_rows = tile_rows * row_count
    map_cols = tile_cols * col_count
    heads = rel_bias.shape[1]
    weights = (qkv_weight, proj_weight, up_weight, down_weight)
    residue_rows = DILATION // row_count
    residue_cols = DILATION // col_count
    block_rows = tile_rows // DILATION
    block_cols = tile_cols // DILATION
    group_rows = block_rows * row_count
    group_cols = block_cols * col_count
    size = group_rows * group_cols

    key_rows = QUERY_ROWS + 2 * HALO
    wide_cols = tile_cols + 2 * HALO
    bias_one = bias_rows(rel_bias[0], QUERY_ROWS, key_rows, tile_cols, wide_cols, HALO, HALO)
    bias_two = bias_rows(rel_bias[1], group_rows, group_rows, group_cols, group_cols, 0, 0)

    rim = padded(padded(tokens, "row", 0, HALO), "col", 1, HALO).reshape(-1, width)
    stream = call_layer(
        functools.partial(local_kernel, (tile_rows, tile_cols, map_rows, map_cols, heads)),
        0,
        (tokens.reshape(-1, width), rim),
        norm_gains,
        bias_one,
        weights,
        rim.shape[0],
        QUERY_ROWS * tile_cols,
        key_rows * wide_cols,
    )
    shaped = stream.reshape(
        block_rows, row_count, residue_rows, block_cols, col_count, residue_cols, width
    )
    shaped = shaped.transpose(1, 4, 2, 5, 0, 3, 6).reshape(
        row_count * col_count, residue_rows, residue_cols, block_rows * block_cols, width
    )
    arrived = lax.all_to_all(shaped, ("row", "col"), split_axis=0, concat_axis=0, tiled=True)
    grouped = arrived.reshape(
        row_count, col_count, residue_rows, residue_cols, block_rows, block_cols, width
    )
    grouped = grouped.transpose(2, 3, 0, 4, 1, 5, 6).reshape(-1, width)
    pack = max(1, 128 // size)
    final = call_layer(
        functools.partial(group_kernel, (group_rows, group_cols, heads, pack)),
        1,
        (grouped,),
        norm_gains,
        bias_two,
        weights,
        grouped.shape[0],
        pack * size,
        pack * size,
    )
    shaped = final.reshape(
        residue_rows, residue_cols, row_count, block_rows, col_count, block_cols, width
    )
    shaped = shaped.transpose(2, 4, 0, 1, 3, 5, 6).reshape(
        row_count * col_count, residue_rows, residue_cols, block_rows * block_cols, width
    )
    arrived = lax.all_to_all(shaped, ("row", "col"), split_axis=0, concat_axis=0, tiled=True)
    restored = arrived.reshape(
        row_count, col_count, residue_rows, residue_cols, block_rows, block_cols, width
    )
    return restored.transpose(4, 0, 2, 5, 1, 3, 6).reshape(tile_rows, tile_cols, width)


def solution(mesh):
    placed = (P("row", "col", None), P(), P(), P(), P(), P(), P())
    return jax.shard_map(
        body, mesh=mesh, in_specs=placed, out_specs=P("row", "col", None), check_vma=False
    )
```

time: 1190 us -> 113 us (0.09); the launches traced: 1170 us -> 113 us
  local copies, waits for them, and re-layouts: 754 us -> 23.8 us
  matrix products: 206 us -> 0 us
  other arithmetic: 165 us -> 2.49 us
  Pallas kernels: 0 us -> 35.9 us
  waiting for transfers between devices: 0.01 us -> 14.6 us
    gather x224 -> x0, local copies, waits for them, and re-layouts: 465 us -> none  [the longest x98 216 us: window_attend(): jnp.take(key_rows, col_start + across, axis=1)]
    dot_general x313 -> x0, matrix products: 206 us -> none  [the longest x112 89.5 us: window_attend(): jnp.einsum('iy,cz,nyz->nic', row_hot, col_hots[across], rel_table, precis...]
    convert_element_type x151 -> x0, local copies, waits for them, and re-layouts: 102 us -> none  [the longest x49 53.2 us: window_attend(): product = query_flat.astype(jnp.float32) * window.astype(jnp.float32)]
    convert_element_type x20 -> x0, other arithmetic: 73.9 us -> none  [the longest x14 70 us: window_attend(): running = running + spread * window.astype(jnp.float32)]
    unnamed x974 -> x10, local copies, waits for them, and re-layouts: 53.9 us -> 1.4 us
    another operation x63 -> x26, local copies, waits for them, and re-layouts: 57.4 us -> 7.38 us  [bias_rows(): return jnp.stack(rows, axis=1).reshape(heads, q_cols, extent * k_cols)]
    pallas_call x0 -> x2, Pallas kernels: none -> 35.9 us  [call_layer(): pl.pallas_call(kernel, grid=(1,), out_shape=jax.ShapeDtypeStruct((rows, w...]
    reshape x57 -> x5, local copies, waits for them, and re-layouts: 34.2 us -> 3.96 us  [the longest x2 1.34 us: body(): stream.reshape(block_rows, row_count, residue_rows, block_cols, col_count...]
  transfers between devices with their start and end apart: 5 -> 5, of which waited for: 0 -> 2; matrix products, arithmetic and copies ran while one was open for 17% -> 13% of each run, Pallas kernels for 0% -> 0%
where the time goes in v1:
time: 113 us
  Pallas kernels  35.9 us (32%)
  local copies, waits for them, and re-layouts  23.8 us (21%)
  blocking collectives  18.4 us (16%)
  starting transfers between devices  17.1 us (15%)
  waiting for transfers between devices  14.6 us (13%)
  other arithmetic  2.49 us (2%)
    pallas_call x2, Pallas kernels, call_layer(): pl.pallas_call(kernel, grid=(1,), out_shape=jax.ShapeDtypeStruct((rows, w...  35.9 us
    all_to_all x1, blocking collectives, body(): lax.all_to_all(shaped, ('row', 'col'), split_axis=0, concat_axis=0, tiled...  18.4 us
    all_to_all x1, waiting for transfers between devices, body(): lax.all_to_all(shaped, ('row', 'col'), split_axis=0, concat_axis=0, tiled...  12.8 us
    all_to_all x1, starting transfers between devices, body(): lax.all_to_all(shaped, ('row', 'col'), split_axis=0, concat_axis=0, tiled...  7.66 us
    another operation x26, local copies, waits for them, and re-layouts, bias_rows(): return jnp.stack(rows, axis=1).reshape(heads, q_cols, extent * k_cols)  7.38 us
    ppermute x2, starting transfers between devices, padded(): lax.ppermute(tail, axis, [(i, i + 1) for i in range(count - 1)])  6.88 us
    slice x26, local copies, waits for them, and re-layouts, bias_rows(): rows = [padded[:, :, start:start + k_cols] for start in starts]  4.22 us
    ppermute x2, starting transfers between devices, padded(): lax.ppermute(head, axis, [(i + 1, i) for i in range(count - 1)])  2.57 us
  transfers between devices with their start and end apart: 5, of which 2 were waited for; matrix products, arithmetic and copies ran while one was open for 13% of the time, Pallas kernels for 0%

profile of v1, /device:TPU:0, one launch (start us, length us, event | category | flops | bytes accessed | tf_op | source)
XLA Modules:
  0.0 112.7 jit_solution(12718035804356602740)
XLA Ops:
  0.0 0.9 fusion.1
  0.9 4.9 %collective-permute-start = (bf16[4,16,512]{2,1,0:T(8,128)(2,1)S(1)}, bf16[4,16,512]{2,1,0:T(8,128)(2,1)S(1)}, u32[]{:S(2)}, u32[]{:S(2)}) collective-permute-start(bf16[4,16,512]{2,1,0:T(8,128)(2,1)S(1)} %get-tuple-element.8), channel_id=1, source_target_pairs={{0,8},{8,16},{16,24},{1,9},{9,17},{17,25},{2,10},{10,18},{18,26},{... | collective-permute-start | bytes 196616 | tf_op jit(solution)/shard_map/ppermute | solution.py:256
  5.8 1.3 %collective-permute-start.1 = (bf16[4,16,512]{2,1,0:T(8,128)(2,1)S(1)}, bf16[4,16,512]{2,1,0:T(8,128)(2,1)S(1)}, u32[]{:S(2)}, u32[]{:S(2)}) collective-permute-start(bf16[4,16,512]{2,1,0:T(8,128)(2,1)S(1)} %get-tuple-element.7), channel_id=1, source_target_pairs={{8,0},{16,8},{24,16},{9,1},{17,9},{25,17},{10,2},{18,10},{26,18},{... | collective-permute-start | bytes 196616 | tf_op jit(solution)/shard_map/ppermute | solution.py:258
  7.1 1.8 %fusion.2 = (f32[1,16,13,13]{1,0,3,2:T(1,128)}, f32[1,16,13,13]{1,0,3,2:T(1,128)S(1)}) fusion(f32[2,16,13,13]{1,0,3,2:T(2,128)} %param.10), kind=kLoop, calls=%fused_computation.36 | loop fusion | bytes 43264 | tf_op jit(solution)/shard_map/slice | solution.py:283
  9.1 1.1 constant_dynamic-update-slice_fusion.1
  10.2 1.8 %collective-permute-done.1 = bf16[4,16,512]{2,1,0:T(8,128)(2,1)S(1)} collective-permute-done((bf16[4,16,512]{2,1,0:T(8,128)(2,1)S(1)}, bf16[4,16,512]{2,1,0:T(8,128)(2,1)S(1)}, u32[]{:S(2)}, u32[]{:S(2)}) %collective-permute-start.1) | collective-permute-done | bytes 65568 | tf_op jit(solution)/shard_map/ppermute | solution.py:258
  12.0 0.8 fusion
  12.8 1.9 %collective-permute-start.2 = (bf16[40,4,512]{2,1,0:T(4,128)(2,1)}, bf16[40,4,512]{2,1,0:T(4,128)(2,1)}, u32[]{:S(2)}, u32[]{:S(2)}) collective-permute-start(bf16[40,4,512]{2,1,0:T(4,128)(2,1)} %get-tuple-element.5), channel_id=1, source_target_pairs={{0,1},{1,2},{2,3},{3,4},{4,5},{5,6},{6,7},{8,9},{9,10},{10,11},{11... | collective-permute-start | bytes 491528 | tf_op jit(solution)/shard_map/ppermute | solution.py:256
  14.8 1.3 %collective-permute-start.3 = (bf16[40,4,512]{2,1,0:T(4,128)(2,1)}, bf16[40,4,512]{2,1,0:T(4,128)(2,1)}, u32[]{:S(2)}, u32[]{:S(2)}) collective-permute-start(bf16[40,4,512]{2,1,0:T(4,128)(2,1)} %get-tuple-element.6), channel_id=1, source_target_pairs={{1,0},{2,1},{3,2},{4,3},{5,4},{6,5},{7,6},{9,8},{10,9},{11,10},{12... | collective-permute-start | bytes 491528 | tf_op jit(solution)/shard_map/ppermute | solution.py:258
  16.1 1.2 %pad_slice_fusion = (f32[16,23,24]{2,0,1:T(8,128)S(1)}, f32[16,23,24]{2,0,1:T(8,128)}, f32[16,23,24]{2,0,1:T(8,128)S(1)}, f32[16,23,24]{2,0,1:T(8,128)S(1)}, f32...) fusion(f32[16,13,13]{2,0,1:T(8,128)S(1)} %multiply_bitcast_fusion.1), kind=kLoop, calls=%fused_computation.1 | loop fusion | bytes 576064 | tf_op jit(solution)/shard_map/slice | solution.py:42
  17.5 1.0 copy.141
  18.5 0.8 stack.105
  19.3 0.8 stack.106
  20.4 0.2 stack.108
  23.2 2.4 %stack.94.bias_ref = f32[16,16,552]{2,1,0:T(8,128)} concatenate(f32[16,1,552]{2,1,0:T(1,128)S(1)} %stack.104, f32[16,1,552]{2,1,0:T(1,128)S(1)} %copy-done.1, f32[16,1,552]{2,1,0:T(1,128)S(1)} %copy-done.2, f32[16,1,552]{2,1,0:T(1,128)S(1)} %stack.107, f32[16,1,552]{2,1,0:T(1,128)S(1)} %stack.108, f32[16,1,552]{2,1,0:T(1,128)S(1)} %stack.109, f32[16,1,552]{2,1,0:T(1,128)S(1)} %stack.110, ...), dimensions={1} | concatenate | bytes 1130496 | tf_op jit(solution)/shard_map/stack | solution.py:43
  25.6 2.5 %pad_maximum_fusion = bf16[40,24,512]{2,1,0:T(8,128)(2,1)} fusion(bf16[40,4,512]{2,1,0:T(4,128)(2,1)} %collective-permute-done.3, bf16[40,16,512]{2,1,0:T(8,128)(2,1)S(1)} %constant_dynamic-update-slice_fusion, bf16[40,4,512]{2,1,0:T(4,128)(2,1)} %collective-permute-done.2), kind=kLoop, calls=%fused_computation | loop fusion | flops 2949120 | bytes 1966080 | tf_op jit(solution)/shard_map/concatenate | solution.py:254
  28.1 20.1 %shard_map.73 = bf16[512,512]{1,0:T(8,128)(2,1)} custom-call(bf16[512,512]{1,0:T(8,128)(2,1)} %bitcast.39, bf16[960,512]{1,0:T(8,128)(2,1)} %bitcast.38, f32[4,512]{1,0:T(4,128)} %gains_ref.3, bf16[2,512,1536]{2,1,0:T(8,128)(2,1)} %qkv_ref.3, f32[16,16,552]{2,1,0:T(8,128)} %stack.94.bias_ref, bf16[2,512,512]{2,1,0:T(8,128)(2,1)} %proj_ref.3, ...), custom_call_target="tpu_custom_call" | custom-call | tf_op jit(solution)/shard_map/pallas_call | solution.py:232
  48.2 1.3 %reshape.86 = bf16[2,4,4,1,8,2,512]{6,5,4,2,1,0,3:T(2,128)(2,1)S(1)} reshape(bf16[512,512]{1,0:T(8,128)(2,1)} %shard_map.73) | data formatting | bytes 1048576 | tf_op jit(solution)/shard_map/reshape | solution.py:297
  49.5 1.3 %copy.173 = bf16[32,4,2,2,512]{4,3,2,1,0:T(2,128)(2,1)} copy(bf16[32,4,2,2,512]{4,0,3,2,1:T(8,128)(2,1)S(1)} %bitcast.42) | data formatting | bytes 1048576 | tf_op jit(solution)/shard_map/reshape | solution.py:300
  50.9 7.7 %all-to-all-start = ((bf16[32,4,2,2,512]{4,3,2,1,0:T(2,128)(2,1)}), bf16[32,4,2,2,512]{4,3,2,1,0:T(2,128)(2,1)S(1)}, u32[]{:S(2)}, u32[]{:S(2)}) async-start(bf16[32,4,2,2,512]{4,3,2,1,0:T(2,128)(2,1)} %copy.173), calls=%async_computation | async-start | bytes 1048576 | tf_op jit(solution)/shard_map/all_to_all | solution.py:303
  58.7 0.3 pad_slice_fusion.16
  60.3 0.7 stack.103.bias_ref
  61.0 12.8 %all-to-all-done = bf16[32,4,2,2,512]{4,3,2,1,0:T(2,128)(2,1)S(1)} async-done(((bf16[32,4,2,2,512]{4,3,2,1,0:T(2,128)(2,1)}), bf16[32,4,2,2,512]{4,3,2,1,0:T(2,128)(2,1)S(1)}, u32[]{:S(2)}, u32[]{:S(2)}) %all-to-all-start) | async-done | bytes 524320 | tf_op jit(solution)/shard_map/all_to_all | solution.py:303
  73.9 0.3 copy.205
  74.2 0.9 copy.175
  75.0 15.8 %shard_map.74 = bf16[512,512]{1,0:T(8,128)(2,1)} custom-call(bf16[512,512]{1,0:T(8,128)(2,1)} %bitcast.40, f32[4,512]{1,0:T(4,128)} %gains_ref.3, bf16[2,512,1536]{2,1,0:T(8,128)(2,1)} %qkv_ref.3, f32[16,8,120]{2,1,0:T(8,128)} %stack.103.bias_ref, bf16[2,512,512]{2,1,0:T(8,128)(2,1)} %proj_ref.3, bf16[2,512,2048]{2,1,0:T(8,128)(2,1)} %up_ref.3, ...), custom_call_target="tpu_custom_call" | custom-call | tf_op jit(solution)/shard_map/pallas_call | solution.py:232
  90.8 1.1 copy.204
  91.9 0.5 copy.194
  92.5 18.4 %all_to_all.10 = bf16[32,4,2,2,512]{4,3,2,1,0:T(2,128)(2,1)S(1)} all-to-all(bf16[32,4,2,2,512]{4,3,2,1,0:T(2,128)(2,1)S(1)} %copy.194), channel_id=1, replica_groups=mesh['row'=4,'col'=8] {'row','col'}, dimensions={0} | all-to-all | bytes 1048576 | tf_op jit(solution)/shard_map/all_to_all | solution.py:326
  110.9 0.3 copy.203
  111.2 0.5 copy.196
  111.7 1.0 reshape.93
  (60 shorter events, 4.7 us)
Async XLA Ops:
  0.9 8.2 %collective-permute-start = (bf16[4,16,512]{2,1,0:T(8,128)(2,1)S(1)}, bf16[4,16,512]{2,1,0:T(8,128)(2,1)S(1)}, u32[]{:S(2)}, u32[]{:S(2)}) collective-permute-start(bf16[4,16,512]{2,1,0:T(8,128)(2,1)S(1)} %get-tuple-element.8), channel_id=1, source_target_pairs={{0,8},{8,16},{16,24},{1,9},{9,17},{17,25},{2,10},{10,18},{18,26},{... | collective-permute-start | bytes 196616 | tf_op jit(solution)/shard_map/ppermute | solution.py:256
  5.8 6.2 %collective-permute-start.1 = (bf16[4,16,512]{2,1,0:T(8,128)(2,1)S(1)}, bf16[4,16,512]{2,1,0:T(8,128)(2,1)S(1)}, u32[]{:S(2)}, u32[]{:S(2)}) collective-permute-start(bf16[4,16,512]{2,1,0:T(8,128)(2,1)S(1)} %get-tuple-element.7), channel_id=1, source_target_pairs={{8,0},{16,8},{24,16},{9,1},{17,9},{25,17},{10,2},{18,10},{26,18},{... | collective-permute-start | bytes 196616 | tf_op jit(solution)/shard_map/ppermute | solution.py:258
  12.8 12.7 %collective-permute-start.2 = (bf16[40,4,512]{2,1,0:T(4,128)(2,1)}, bf16[40,4,512]{2,1,0:T(4,128)(2,1)}, u32[]{:S(2)}, u32[]{:S(2)}) collective-permute-start(bf16[40,4,512]{2,1,0:T(4,128)(2,1)} %get-tuple-element.5), channel_id=1, source_target_pairs={{0,1},{1,2},{2,3},{3,4},{4,5},{5,6},{6,7},{8,9},{9,10},{10,11},{11... | collective-permute-start | bytes 491528 | tf_op jit(solution)/shard_map/ppermute | solution.py:256
  14.8 10.8 %collective-permute-start.3 = (bf16[40,4,512]{2,1,0:T(4,128)(2,1)}, bf16[40,4,512]{2,1,0:T(4,128)(2,1)}, u32[]{:S(2)}, u32[]{:S(2)}) collective-permute-start(bf16[40,4,512]{2,1,0:T(4,128)(2,1)} %get-tuple-element.6), channel_id=1, source_target_pairs={{1,0},{2,1},{3,2},{4,3},{5,4},{6,5},{7,6},{9,8},{10,9},{11,10},{12... | collective-permute-start | bytes 491528 | tf_op jit(solution)/shard_map/ppermute | solution.py:258
  21.6 1.6 %copy-start.1 = (f32[16,1,552]{2,1,0:T(1,128)S(1)}, f32[16,1,552]{2,1,0:T(1,128)}, u32[]{:S(2)}) copy-start(f32[16,1,552]{2,1,0:T(1,128)} %stack.105) | copy-start | bytes 105988
  21.6 1.6 %copy-start.2 = (f32[16,1,552]{2,1,0:T(1,128)S(1)}, f32[16,1,552]{2,1,0:T(1,128)}, u32[]{:S(2)}) copy-start(f32[16,1,552]{2,1,0:T(1,128)} %stack.106) | copy-start | bytes 105988
  48.2 10.4 %copy-start = (f32[1,16,13,13]{1,0,3,2:T(1,128)S(1)}, f32[1,16,13,13]{1,0,3,2:T(1,128)}, u32[]{:S(2)}) copy-start(f32[1,16,13,13]{1,0,3,2:T(1,128)} %get-tuple-element.9) | copy-start | bytes 32452
  50.9 23.0 %all-to-all-start = ((bf16[32,4,2,2,512]{4,3,2,1,0:T(2,128)(2,1)}), bf16[32,4,2,2,512]{4,3,2,1,0:T(2,128)(2,1)S(1)}, u32[]{:S(2)}, u32[]{:S(2)}) async-start(bf16[32,4,2,2,512]{4,3,2,1,0:T(2,128)(2,1)} %copy.173), calls=%async_computation | async-start | bytes 1048576 | tf_op jit(solution)/shard_map/all_to_all | solution.py:303

commit v2 on v1

v2 whole, which is shorter than its diff:
```python
import functools
import math

import jax
import jax.numpy as jnp
from jax import lax
from jax.experimental import pallas as pl
from jax.experimental.pallas import tpu as pltpu
from jax.sharding import PartitionSpec as P

DILATION = 16
REACH = 6
HALO = 4
QUERY_ROWS = 8
MASKED = -1e30
LOG2E = 1.4426950408889634
VMEM_BYTES = 56 * 1024 * 1024


def layer_norm(values, gain):
    values_f = values.astype(jnp.float32)
    mean_value = jnp.mean(values_f, axis=-1, keepdims=True)
    centred = values_f - mean_value
    variance = jnp.mean(centred * centred, axis=-1, keepdims=True)
    return (centred * lax.rsqrt(variance + 1e-05) * gain).astype(jnp.bfloat16)


def dot(left, right):
    return jnp.dot(left, right, preferred_element_type=jnp.float32)


def fill_bias(rel_ref, rows_ref, full_ref, q_rows, k_rows, row_off, k_cols, col_places, first_key, groups):
    heads, entries = rel_ref.shape
    classes = math.isqrt(entries)
    q_cols = rows_ref.shape[1] // heads
    extent = q_rows + k_rows - 1
    before = q_rows - 1 + row_off - REACH
    chunks = -(-extent * k_cols // 128)
    width = chunks * 128
    place = lax.broadcasted_iota(jnp.int32, (1, width), 1)
    entry = lax.broadcasted_iota(jnp.int32, (entries, 1), 0)
    across = place // k_cols
    key_col = col_places(place - across * k_cols)
    down = across - before
    table = rel_ref[...] * LOG2E
    for j in range(q_cols):
        over = key_col - j + REACH
        known = (down >= 0) & (down < classes) & (over >= 0) & (over < classes)
        target = jnp.where(known, down * classes + over, -1)
        hot = (entry == target).astype(jnp.float32)
        found = jnp.dot(
            table, hot, precision=lax.Precision.HIGHEST, preferred_element_type=jnp.float32
        )
        for c in range(chunks):
            rows_ref[c, j * heads : (j + 1) * heads, :] = found[:, c * 128 : (c + 1) * 128]
    n_key = k_rows * k_cols
    for n in range(heads):
        strips = jnp.concatenate(
            [rows_ref[c, pl.ds(n, q_cols, stride=heads), :] for c in range(chunks)], axis=1
        )
        for i in range(q_rows):
            start = (q_rows - 1 - i) * k_cols
            strip = jnp.concatenate([strips[:, start : start + n_key]] * groups, axis=1)
            for t in range(groups):
                first = t * n_key + i * q_cols
                full_ref[n, first : first + q_cols, first_key : first_key + groups * n_key] = strip


def slot_places(index, shape):
    tile_cols, residue_rows, residue_cols, block_rows, block_cols, col_count, slot = shape
    row = index // tile_cols
    col = index - row * tile_cols
    row_block = row // DILATION
    col_block = col // DILATION
    row, col = row - row_block * DILATION, col - col_block * DILATION
    peer_row = row // residue_rows
    peer_col = col // residue_cols
    inner = (row - peer_row * residue_rows) * residue_cols + col - peer_col * residue_cols
    inner = (inner * block_rows + row_block) * block_cols + col_block
    return (peer_row * col_count + peer_col) * slot + inner


def group_places(index, shape):
    _, residue_rows, residue_cols, block_rows, block_cols, col_count, slot, row_count = shape
    used = residue_rows * residue_cols * block_rows * block_cols
    peer = index // slot
    inner = index - peer * slot
    peer_row = peer // col_count
    peer_col = peer - peer_row * col_count
    rest = inner // block_cols
    col_block = inner - rest * block_cols
    residue = rest // block_rows
    row_block = rest - residue * block_rows
    place = residue * (block_rows * row_count) + peer_row * block_rows + row_block
    place = place * (block_cols * col_count) + peer_col * block_cols + col_block
    return jnp.where(inner < used, place, -1)


def column(count):
    return lax.broadcasted_iota(jnp.int32, (count, 1), 0)


def line(count):
    return lax.broadcasted_iota(jnp.int32, (1, count), 1)


def one_hot(left, right):
    return jnp.where(left == right, 1.0, 0.0).astype(jnp.bfloat16)


def in_window(query, key, extent):
    start = jnp.clip(query - 3, 0, extent - 7)
    return (key >= start) & (key < start + 7)


def head_lanes(lanes, head_size):
    lane = lax.broadcasted_iota(jnp.int32, (1, lanes), 1)
    return [(lane // head_size) == h for h in range(lanes // head_size)]


def attend(queries, keys, values, bias, mask, head_size):
    count, lanes = queries.shape
    picks = head_lanes(lanes, head_size)
    zero = jnp.zeros_like(queries)
    stacked = jnp.concatenate([jnp.where(pick, queries, zero) for pick in picks], axis=0)
    scores = lax.dot_general(
        stacked, keys, (((1,), (1,)), ((), ())), preferred_element_type=jnp.float32
    )
    scores = scores.reshape(len(picks), count, keys.shape[0]) + bias
    if mask is not None:
        scores = scores + mask[None]
    peak = jnp.max(scores, axis=-1, keepdims=True)
    weights = jnp.exp2(scores - peak).astype(jnp.bfloat16)
    wide = jnp.concatenate([values, jnp.ones_like(values)], axis=1)
    summed = dot(weights.reshape(len(picks) * count, keys.shape[0]), wide)
    ratio = summed[:, :lanes] / summed[:, lanes:]
    result = ratio[:count]
    for h in range(1, len(picks)):
        result = jnp.where(picks[h], ratio[h * count : (h + 1) * count], result)
    return result.astype(jnp.bfloat16)


def finish(att_ref, x_ref, gain, proj_ref, up_ref, down_ref, out_ref, chunk):
    width = x_ref.shape[1]
    hidden_width = up_ref.shape[1]
    part = math.gcd(hidden_width, 512)

    def step(index, carry):
        rows = pl.ds(pl.multiple_of(index * chunk, chunk), chunk)
        mixed = (dot(att_ref[rows, :], proj_ref[...]) + x_ref[rows, :].astype(jnp.float32)).astype(
            jnp.bfloat16
        )
        normed = layer_norm(mixed, gain)
        total = mixed.astype(jnp.float32)
        for first in range(0, hidden_width, part):
            hidden = jax.nn.gelu(dot(normed, up_ref[:, first : first + part]), approximate=True)
            total = total + dot(hidden.astype(jnp.bfloat16), down_ref[first : first + part, :])
        out_ref[rows, :] = total.astype(jnp.bfloat16)
        return carry

    lax.fori_loop(0, x_ref.shape[0] // chunk, step, 0)


def project(src_ref, gain, weight, dst_ref, scale, chunk):
    def step(index, carry):
        rows = pl.ds(pl.multiple_of(index * chunk, chunk), chunk)
        result = dot(layer_norm(src_ref[rows, :], gain), weight)
        if scale is not None:
            result = result * scale
        dst_ref[rows, :] = result.astype(jnp.bfloat16)
        return carry

    lax.fori_loop(0, src_ref.shape[0] // chunk, step, 0)


def local_kernel(
    geometry, x_ref, above_ref, below_ref, left_ref, right_ref, gains_ref, qkv_ref, rel_ref,
    proj_ref, up_ref, down_ref, out_ref, q_ref, kv_ref, full_ref, att_ref, bias_ref, pad_ref,
):
    tile_rows, tile_cols, map_rows, map_cols, heads, places = geometry
    tokens, width = x_ref.shape
    head_size = width // heads
    lanes = 128
    per = lanes // head_size
    key_rows = QUERY_ROWS + 2 * HALO
    n_query = QUERY_ROWS * tile_cols
    scale = head_size ** (-0.5) * LOG2E
    gain = gains_ref[0:1, :]
    rim = HALO * tile_cols
    side = (tile_rows + 2 * HALO) * HALO
    own = tokens + 2 * rim
    pad_ref[0:rim, :] = above_ref[...]
    pad_ref[rim : rim + tokens, :] = x_ref[...]
    pad_ref[rim + tokens : own, :] = below_ref[...]
    pad_ref[own : own + side, :] = left_ref[...]
    pad_ref[own + side :, :] = right_ref[...]
    sets = (
        (0, tile_cols, 0, lambda col: col),
        (own, HALO, key_rows * tile_cols, lambda col: col - HALO),
        (own + side, HALO, key_rows * (tile_cols + HALO), lambda col: col + tile_cols),
    )
    for _, k_cols, first_key, col_places in sets:
        fill_bias(
            rel_ref, bias_ref, full_ref, QUERY_ROWS, key_rows, HALO, k_cols, col_places, first_key, 1
        )
    project(x_ref, gain, qkv_ref[:, :width], q_ref, scale, 256)
    project(pad_ref, gain, qkv_ref[:, width:], kv_ref, None, math.gcd(pad_ref.shape[0], 320))
    first_row = lax.axis_index("row") * tile_rows
    first_col = lax.axis_index("col") * tile_cols
    query = column(n_query)
    query_row = query // tile_cols
    query_col = first_col + query - query_row * tile_cols
    seen_cols, key_row_list = [], []
    for _, k_cols, _, col_places in sets:
        key = line(key_rows * k_cols)
        key_row = key // k_cols
        key_row_list.append(key_row)
        key_col = first_col + col_places(key - key_row * k_cols)
        seen_cols.append(in_window(query_col, key_col, map_cols))

    def step(block, carry):
        top = first_row + block * QUERY_ROWS
        masks = [
            jnp.where(col_seen & in_window(top + query_row, top + key_row - HALO, map_rows), 0.0, MASKED)
            for col_seen, key_row in zip(seen_cols, key_row_list)
        ]
        mask = jnp.concatenate(masks, axis=1).astype(jnp.float32)
        q_rows = pl.ds(pl.multiple_of(block * n_query, n_query), n_query)
        k_rows = []
        for base, k_cols, _, _ in sets:
            stride = QUERY_ROWS * k_cols
            k_rows.append(pl.ds(pl.multiple_of(base + block * stride, 16), key_rows * k_cols))
        for g in range(width // lanes):
            cols = slice(g * lanes, (g + 1) * lanes)
            v_cols = slice(width + g * lanes, width + (g + 1) * lanes)
            att_ref[q_rows, cols] = attend(
                q_ref[q_rows, cols],
                jnp.concatenate([kv_ref[rows, cols] for rows in k_rows], axis=0),
                jnp.concatenate([kv_ref[rows, v_cols] for rows in k_rows], axis=0),
                full_ref[g * per : (g + 1) * per],
                mask,
                head_size,
            )
        return carry

    lax.fori_loop(0, tile_rows // QUERY_ROWS, step, 0)
    finish(att_ref, x_ref, gains_ref[1:2, :], proj_ref, up_ref, down_ref, q_ref, 256)
    hot = one_hot(column(out_ref.shape[0]), slot_places(line(tokens), places[:7]))
    out_ref[...] = dot(hot, q_ref[...]).astype(jnp.bfloat16)


def group_kernel(
    geometry, in_ref, gains_ref, qkv_ref, rel_ref, proj_ref, up_ref, down_ref, out_ref,
    q_ref, kv_ref, full_ref, att_ref, bias_ref, x_ref,
):
    group_rows, group_cols, heads, pack, places = geometry
    tokens, width = x_ref.shape
    arrivals = in_ref.shape[0]
    head_size = width // heads
    lanes = 128
    per = lanes // head_size
    size = group_rows * group_cols
    n_query = pack * size
    scale = head_size ** (-0.5) * LOG2E
    gain = gains_ref[2:3, :]
    hot = one_hot(column(tokens), group_places(line(arrivals), places))
    x_ref[...] = dot(hot, in_ref[...]).astype(jnp.bfloat16)
    query = column(n_query)
    key = line(n_query)
    query_row, key_row = query // group_cols, key // group_cols
    query_col, key_col = query - query_row * group_cols, key - key_row * group_cols
    query_group, key_group = query // size, key // size
    seen = (
        (query_group == key_group)
        & in_window(query_row - query_group * group_rows, key_row - key_group * group_rows, group_rows)
        & in_window(query_col, key_col, group_cols)
    )
    fill_bias(
        rel_ref, bias_ref, full_ref, group_rows, group_rows, 0, group_cols, lambda col: col, 0, pack
    )
    for n in range(heads):
        full_ref[n] = jnp.where(seen, full_ref[n], MASKED)
    project(x_ref, gain, qkv_ref[:, :width], q_ref, scale, 256)
    project(x_ref, gain, qkv_ref[:, width:], kv_ref, None, 256)

    def step(block, carry):
        rows = pl.ds(pl.multiple_of(block * n_query, n_query), n_query)
        for g in range(width // lanes):
            cols = slice(g * lanes, (g + 1) * lanes)
            v_cols = slice(width + g * lanes, width + (g + 1) * lanes)
            att_ref[rows, cols] = attend(
                q_ref[rows, cols],
                kv_ref[rows, cols],
                kv_ref[rows, v_cols],
                full_ref[g * per : (g + 1) * per],
                None,
                head_size,
            )
        return carry

    lax.fori_loop(0, tokens // n_query, step, 0)
    finish(att_ref, x_ref, gains_ref[3:4, :], proj_ref, up_ref, down_ref, q_ref, 256)
    back = one_hot(group_places(column(arrivals), places), line(tokens))
    out_ref[...] = dot(back, q_ref[...]).astype(jnp.bfloat16)


def place_kernel(places, in_ref, out_ref):
    hot = one_hot(slot_places(column(out_ref.shape[0]), places[:7]), line(in_ref.shape[0]))
    out_ref[...] = dot(hot, in_ref[...]).astype(jnp.bfloat16)


def whole(array):
    return pl.BlockSpec(array.shape, lambda i: (0,) * array.ndim)


def one_layer(array, layer):
    return pl.BlockSpec((None,) + array.shape[1:], lambda i: (layer,) + (0,) * (array.ndim - 1))


def call_layer(kernel, layer, acts, gains, rel, weights, out_rows, tokens, key_count, n_query, n_key, bias, pad):
    qkv, proj, up, down = weights
    width = acts[0].shape[1]
    heads = rel.shape[1]
    q_cols, bias_width = bias
    return pl.pallas_call(
        kernel,
        grid=(1,),
        out_shape=jax.ShapeDtypeStruct((out_rows, width), jnp.bfloat16),
        in_specs=[whole(act) for act in acts]
        + [whole(gains), one_layer(qkv, layer), one_layer(rel, layer)]
        + [one_layer(weight, layer) for weight in (proj, up, down)],
        out_specs=pl.BlockSpec((out_rows, width), lambda i: (0, 0)),
        scratch_shapes=[
            pltpu.VMEM((tokens, width), jnp.bfloat16),
            pltpu.VMEM((key_count, 2 * width), jnp.bfloat16),
            pltpu.VMEM((heads, n_query, n_key), jnp.float32),
            pltpu.VMEM((tokens, width), jnp.bfloat16),
            pltpu.VMEM((-(-bias_width // 128), q_cols * heads, 128), jnp.float32),
            pltpu.VMEM((pad, width), jnp.bfloat16),
        ],
        compiler_params=pltpu.CompilerParams(vmem_limit_bytes=VMEM_BYTES),
    )(*acts, gains, qkv, rel, proj, up, down)


def from_both(cells, axis, dim, width):
    count = lax.axis_size(axis)
    head = lax.slice_in_dim(cells, 0, width, axis=dim)
    tail = lax.slice_in_dim(cells, cells.shape[dim] - width, cells.shape[dim], axis=dim)
    return (
        lax.ppermute(tail, axis, [(i, i + 1) for i in range(count - 1)]),
        lax.ppermute(head, axis, [(i + 1, i) for i in range(count - 1)]),
    )


def body(tokens, norm_gains, qkv_weight, rel_bias, proj_weight, up_weight, down_weight):
    tile_rows, tile_cols, width = tokens.shape
    row_count = lax.axis_size("row")
    col_count = lax.axis_size("col")
    heads = rel_bias.shape[1]
    rel = rel_bias.reshape(rel_bias.shape[0], heads, -1)
    weights = (qkv_weight, proj_weight, up_weight, down_weight)
    residue_rows = DILATION // row_count
    residue_cols = DILATION // col_count
    block_rows = tile_rows // DILATION
    block_cols = tile_cols // DILATION
    group_rows = block_rows * row_count
    group_cols = block_cols * col_count
    size = group_rows * group_cols
    peers = row_count * col_count
    count = tile_rows * tile_cols
    slot = -(-(count // peers) // 16) * 16
    places = (
        tile_cols, residue_rows, residue_cols, block_rows, block_cols, col_count, slot, row_count
    )

    key_rows = QUERY_ROWS + 2 * HALO
    above, below = from_both(tokens, "row", 0, HALO)
    edges = jnp.concatenate(
        [
            jnp.concatenate([above[:, :HALO], tokens[:, :HALO], below[:, :HALO]], axis=0),
            jnp.concatenate([above[:, -HALO:], tokens[:, -HALO:], below[:, -HALO:]], axis=0),
        ],
        axis=1,
    )
    left, right = from_both(edges, "col", 1, HALO)
    flat = [piece.reshape(-1, width) for piece in (tokens, above, below, left, right)]
    pad = sum(piece.shape[0] for piece in flat)
    wide_cols = tile_cols + 2 * HALO
    sent = call_layer(
        functools.partial(
            local_kernel,
            (tile_rows, tile_cols, tile_rows * row_count, tile_cols * col_count, heads, places),
        ),
        0,
        flat,
        norm_gains,
        rel,
        weights,
        peers * slot,
        count,
        pad,
        QUERY_ROWS * tile_cols,
        key_rows * wide_cols,
        (tile_cols, (QUERY_ROWS + key_rows - 1) * tile_cols),
        pad,
    )
    arrived = lax.all_to_all(
        sent.reshape(peers, slot, width), ("row", "col"), split_axis=0, concat_axis=0, tiled=True
    ).reshape(-1, width)
    pack = max(1, 128 // size)
    sent = call_layer(
        functools.partial(group_kernel, (group_rows, group_cols, heads, pack, places)),
        1,
        [arrived],
        norm_gains,
        rel,
        weights,
        peers * slot,
        count,
        count,
        pack * size,
        pack * size,
        (group_cols, (2 * group_rows - 1) * group_cols),
        count,
    )
    arrived = lax.all_to_all(
        sent.reshape(peers, slot, width), ("row", "col"), split_axis=0, concat_axis=0, tiled=True
    ).reshape(-1, width)
    placed = pl.pallas_call(
        functools.partial(place_kernel, places),
        out_shape=jax.ShapeDtypeStruct((count, width), jnp.bfloat16),
        compiler_params=pltpu.CompilerParams(vmem_limit_bytes=VMEM_BYTES),
    )(arrived)
    return placed.reshape(tile_rows, tile_cols, width)


def solution(mesh):
    placed = (P("row", "col", None), P(), P(), P(), P(), P(), P())
    return jax.shard_map(
        body, mesh=mesh, in_specs=placed, out_specs=P("row", "col", None), check_vma=False
    )
```

time: 113 us -> 107 us (0.947)
  blocking collectives: 18.4 us -> 44.5 us
  local copies, waits for them, and re-layouts: 23.8 us -> 5.08 us
  waiting for transfers between devices: 14.6 us -> 2.51 us
  Pallas kernels: 35.9 us -> 44.9 us
  starting transfers between devices: 17.1 us -> 9.44 us
  other arithmetic: 2.49 us -> 0.24 us
    all_to_all x1 -> x2, blocking collectives: 18.4 us -> 44.5 us  [body(): lax.all_to_all(sent.reshape(peers, slot, width), ('row', 'col'), split_ax...]
    all_to_all x1 -> x0, waiting for transfers between devices: 12.8 us -> none  [body(): lax.all_to_all(shaped, ('row', 'col'), split_axis=0, concat_axis=0, tiled...]
    pallas_call x2 -> x3, Pallas kernels: 35.9 us -> 44.9 us  [the longest x2 42.1 us: call_layer(): pl.pallas_call(kernel, grid=(1,), out_shape=jax.ShapeDtypeStruct((out_row...]
    all_to_all x1 -> x0, starting transfers between devices: 7.66 us -> none  [body(): lax.all_to_all(shaped, ('row', 'col'), split_axis=0, concat_axis=0, tiled...]
    another operation x26 -> x0, local copies, waits for them, and re-layouts: 7.38 us -> none  [bias_rows(): return jnp.stack(rows, axis=1).reshape(heads, q_cols, extent * k_cols)]
    slice x29 -> x4, local copies, waits for them, and re-layouts: 7.74 us -> 2.05 us  [the longest x1 1.14 us: body(): tokens[:, :HALO]]
    reshape x6 -> x3, local copies, waits for them, and re-layouts: 5.29 us -> 3.03 us  [the longest x1 1.64 us: body(): rel = rel_bias.reshape(rel_bias.shape[0], heads, -1)]
    concatenate x1 -> x2, other arithmetic: 2.47 us -> 0.24 us  [the longest x1 0.12 us: body(): jnp.concatenate([above[:, -HALO:], tokens[:, -HALO:], below[:, -HALO:]],...]
  transfers between devices with their start and end apart: 5 -> 4, of which waited for: 2 -> 2; matrix products, arithmetic and copies ran while one was open for 13% -> 3% of each run, Pallas kernels for 0% -> 0%
where the time goes in v2:
time: 107 us
  Pallas kernels  44.9 us (42%)
  blocking collectives  44.5 us (42%)
  starting transfers between devices  9.44 us (9%)
  local copies, waits for them, and re-layouts  5.08 us (5%)
  waiting for transfers between devices  2.51 us (2%)
    all_to_all x2, blocking collectives, body(): lax.all_to_all(sent.reshape(peers, slot, width), ('row', 'col'), split_ax...  44.5 us
    pallas_call x2, Pallas kernels, call_layer(): pl.pallas_call(kernel, grid=(1,), out_shape=jax.ShapeDtypeStruct((out_row...  42.1 us
    ppermute x2, starting transfers between devices, from_both(): lax.ppermute(tail, axis, [(i, i + 1) for i in range(count - 1)])  6.86 us
    pallas_call x1, Pallas kernels, body(): pl.pallas_call(functools.partial(place_kernel, places), out_shape=jax.Sha...  2.79 us
    ppermute x2, starting transfers between devices, from_both(): lax.ppermute(head, axis, [(i + 1, i) for i in range(count - 1)])  2.58 us
  transfers between devices with their start and end apart: 4, of which 2 were waited for; matrix products, arithmetic and copies ran while one was open for 3% of the time, Pallas kernels for 0%

profile of v2, /device:TPU:0, one launch (start us, length us, event | category | flops | bytes accessed | tf_op | source)
XLA Modules:
  0.0 106.8 jit_solution(15608519786540376253)
XLA Ops:
  0.0 0.9 fusion.1
  0.9 1.3 %collective-permute-start.1 = (bf16[4,16,512]{2,1,0:T(8,128)(2,1)S(1)}, bf16[4,16,512]{2,1,0:T(8,128)(2,1)S(1)}, u32[]{:S(2)}, u32[]{:S(2)}) collective-permute-start(bf16[4,16,512]{2,1,0:T(8,128)(2,1)S(1)} %get-tuple-element.7), channel_id=1, source_target_pairs={{8,0},{16,8},{24,16},{9,1},{17,9},{25,17},{10,2},{18,10},{26,18},{... | collective-permute-start | bytes 196616 | tf_op jit(solution)/shard_map/ppermute | solution.py:351
  2.2 5.6 %collective-permute-start = (bf16[4,16,512]{2,1,0:T(8,128)(2,1)S(1)}, bf16[4,16,512]{2,1,0:T(8,128)(2,1)S(1)}, u32[]{:S(2)}, u32[]{:S(2)}) collective-permute-start(bf16[4,16,512]{2,1,0:T(8,128)(2,1)S(1)} %get-tuple-element.8), channel_id=1, source_target_pairs={{0,8},{8,16},{16,24},{1,9},{9,17},{17,25},{2,10},{10,18},{18,26},{... | collective-permute-start | bytes 196616 | tf_op jit(solution)/shard_map/ppermute | solution.py:350
  7.8 1.1 %fusion = (bf16[32,4,512]{2,1,0:T(4,128)(2,1)S(1)}, bf16[32,4,512]{2,1,0:T(4,128)(2,1)S(1)}) fusion(bf16[32,16,512]{2,1,0:T(8,128)(2,1)} %param.7), kind=kLoop, calls=%fused_computation.2 | loop fusion | bytes 524288 | tf_op jit(solution)/shard_map/slice | solution.py:380
  8.9 0.0 collective-permute-done.1
  8.9 0.0 copy-start
  8.9 0.7 collective-permute-done
  9.6 0.0 copy-start.1
  9.7 0.1 pad_maximum_fusion
  9.8 1.3 %collective-permute-start.2 = (bf16[40,4,512]{2,1,0:T(4,128)(2,1)S(1)}, bf16[40,4,512]{2,1,0:T(4,128)(2,1)S(1)}, u32[]{:S(2)}, u32[]{:S(2)}) collective-permute-start(bf16[40,4,512]{2,1,0:T(4,128)(2,1)S(1)} %pad_maximum_fusion), channel_id=1, source_target_pairs={{0,1},{1,2},{2,3},{3,4},{4,5},{5,6},{6,7},{8,9},{9,10},{10,11},{11... | collective-permute-start | bytes 491528 | tf_op jit(solution)/shard_map/ppermute | solution.py:350
  11.1 0.1 pad_maximum_fusion.1
  11.2 1.3 %collective-permute-start.3 = (bf16[40,4,512]{2,1,0:T(4,128)(2,1)S(1)}, bf16[40,4,512]{2,1,0:T(4,128)(2,1)S(1)}, u32[]{:S(2)}, u32[]{:S(2)}) collective-permute-start(bf16[40,4,512]{2,1,0:T(4,128)(2,1)S(1)} %pad_maximum_fusion.1), channel_id=1, source_target_pairs={{1,0},{2,1},{3,2},{4,3},{5,4},{6,5},{7,6},{9,8},{10,9},{11,10},{12... | collective-permute-start | bytes 491528 | tf_op jit(solution)/shard_map/ppermute | solution.py:351
  12.5 1.6 %copy.10.rel_ref = f32[2,16,169]{2,1,0:T(8,128)} copy(f32[2,16,169]{1,0,2:T(2,128)} %bitcast.14) | data formatting | bytes 43264 | tf_op jit(solution)/shard_map/reshape | solution.py:360
  14.2 0.0 collective-permute-done.2
  14.2 0.7 reshape.36.left_ref
  14.9 1.8 %collective-permute-done.3 = bf16[40,4,512]{2,1,0:T(4,128)(2,1)S(1)} collective-permute-done((bf16[40,4,512]{2,1,0:T(4,128)(2,1)S(1)}, bf16[40,4,512]{2,1,0:T(4,128)(2,1)S(1)}, u32[]{:S(2)}, u32[]{:S(2)}) %collective-permute-start.3) | collective-permute-done | bytes 163872 | tf_op jit(solution)/shard_map/ppermute | solution.py:351
  16.7 0.7 reshape.37.right_ref
  17.4 0.0 copy-done
  17.4 0.0 copy-done.1
  17.4 24.8 %shard_map.73 = bf16[512,512]{1,0:T(8,128)(2,1)} custom-call(bf16[512,512]{1,0:T(8,128)(2,1)} %bitcast.13, bf16[64,512]{1,0:T(8,128)(2,1)} %bitcast.16, bf16[64,512]{1,0:T(8,128)(2,1)} %bitcast.15, bf16[160,512]{1,0:T(8,128)(2,1)} %reshape.36.left_ref, bf16[160,512]{1,0:T(8,128)(2,1)} %reshape.37.right_ref, f32[4,512]{1,0:T(4,128)} %gains_ref.3, ...), custom_call_target="tpu_custom_call" | custom-call | tf_op jit(solution)/shard_map/pallas_call | solution.py:325
  42.2 25.7 %all_to_all.10 = bf16[32,16,512]{2,1,0:T(8,128)(2,1)} all-to-all(bf16[32,16,512]{2,1,0:T(8,128)(2,1)} %bitcast.9), channel_id=1, replica_groups=mesh['row'=4,'col'=8] {'row','col'}, dimensions={0} | all-to-all | bytes 1048576 | tf_op jit(solution)/shard_map/all_to_all | solution.py:407
  67.8 17.3 %shard_map.74 = bf16[512,512]{1,0:T(8,128)(2,1)} custom-call(bf16[512,512]{1,0:T(8,128)(2,1)} %bitcast.10, f32[4,512]{1,0:T(4,128)} %gains_ref.3, bf16[2,512,1536]{2,1,0:T(8,128)(2,1)} %qkv_ref.3, f32[2,16,169]{2,1,0:T(8,128)} %copy.10.rel_ref, bf16[2,512,512]{2,1,0:T(8,128)(2,1)} %proj_ref.3, bf16[2,512,2048]{2,1,0:T(8,128)(2,1)} %up_ref.3, ...), custom_call_target="tpu_custom_call" | custom-call | tf_op jit(solution)/shard_map/pallas_call | solution.py:325
  85.1 18.9 %all_to_all.11 = bf16[32,16,512]{2,1,0:T(8,128)(2,1)} all-to-all(bf16[32,16,512]{2,1,0:T(8,128)(2,1)} %bitcast.11), channel_id=1, replica_groups=mesh['row'=4,'col'=8] {'row','col'}, dimensions={0} | all-to-all | bytes 1048576 | tf_op jit(solution)/shard_map/all_to_all | solution.py:426
  104.0 2.8 %shard_map.75 = bf16[512,512]{1,0:T(8,128)(2,1)} custom-call(bf16[512,512]{1,0:T(8,128)(2,1)} %bitcast.12), custom_call_target="tpu_custom_call" | custom-call | tf_op jit(solution)/shard_map/pallas_call | solution.py:429
  (2 shorter events, 0.0 us)
Async XLA Ops:
  0.9 8.0 %collective-permute-start.1 = (bf16[4,16,512]{2,1,0:T(8,128)(2,1)S(1)}, bf16[4,16,512]{2,1,0:T(8,128)(2,1)S(1)}, u32[]{:S(2)}, u32[]{:S(2)}) collective-permute-start(bf16[4,16,512]{2,1,0:T(8,128)(2,1)S(1)} %get-tuple-element.7), channel_id=1, source_target_pairs={{8,0},{16,8},{24,16},{9,1},{17,9},{25,17},{10,2},{18,10},{26,18},{... | collective-permute-start | bytes 196616 | tf_op jit(solution)/shard_map/ppermute | solution.py:351
  2.2 7.5 %collective-permute-start = (bf16[4,16,512]{2,1,0:T(8,128)(2,1)S(1)}, bf16[4,16,512]{2,1,0:T(8,128)(2,1)S(1)}, u32[]{:S(2)}, u32[]{:S(2)}) collective-permute-start(bf16[4,16,512]{2,1,0:T(8,128)(2,1)S(1)} %get-tuple-element.8), channel_id=1, source_target_pairs={{0,8},{8,16},{16,24},{1,9},{9,17},{17,25},{2,10},{10,18},{18,26},{... | collective-permute-start | bytes 196616 | tf_op jit(solution)/shard_map/ppermute | solution.py:350
  8.9 8.5 %copy-start = (bf16[4,16,512]{2,1,0:T(8,128)(2,1)}, bf16[4,16,512]{2,1,0:T(8,128)(2,1)S(1)}, u32[]{:S(2)}) copy-start(bf16[4,16,512]{2,1,0:T(8,128)(2,1)S(1)} %collective-permute-done.1) | copy-start | bytes 196612
  9.6 7.7 %copy-start.1 = (bf16[4,16,512]{2,1,0:T(8,128)(2,1)}, bf16[4,16,512]{2,1,0:T(8,128)(2,1)S(1)}, u32[]{:S(2)}) copy-start(bf16[4,16,512]{2,1,0:T(8,128)(2,1)S(1)} %collective-permute-done) | copy-start | bytes 196612
  9.8 4.4 %collective-permute-start.2 = (bf16[40,4,512]{2,1,0:T(4,128)(2,1)S(1)}, bf16[40,4,512]{2,1,0:T(4,128)(2,1)S(1)}, u32[]{:S(2)}, u32[]{:S(2)}) collective-permute-start(bf16[40,4,512]{2,1,0:T(4,128)(2,1)S(1)} %pad_maximum_fusion), channel_id=1, source_target_pairs={{0,1},{1,2},{2,3},{3,4},{4,5},{5,6},{6,7},{8,9},{9,10},{10,11},{11... | collective-permute-start | bytes 491528 | tf_op jit(solution)/shard_map/ppermute | solution.py:350
  11.2 5.4 %collective-permute-start.3 = (bf16[40,4,512]{2,1,0:T(4,128)(2,1)S(1)}, bf16[40,4,512]{2,1,0:T(4,128)(2,1)S(1)}, u32[]{:S(2)}, u32[]{:S(2)}) collective-permute-start(bf16[40,4,512]{2,1,0:T(4,128)(2,1)S(1)} %pad_maximum_fusion.1), channel_id=1, source_target_pairs={{1,0},{2,1},{3,2},{4,3},{5,4},{6,5},{7,6},{9,8},{10,9},{11,10},{12... | collective-permute-start | bytes 491528 | tf_op jit(solution)/shard_map/ppermute | solution.py:351

commit v3 on v2

v3 whole, which is shorter than its diff:
```python
import functools
import math

import jax
import jax.numpy as jnp
from jax import lax
from jax.experimental import pallas as pl
from jax.experimental.pallas import tpu as pltpu
from jax.sharding import PartitionSpec as P

DILATION = 16
REACH = 6
HALO = 4
QUERY_ROWS = 8
MASKED = -1e30
LOG2E = 1.4426950408889634
VMEM_BYTES = 56 * 1024 * 1024


def layer_norm(values, gain):
    values_f = values.astype(jnp.float32)
    mean_value = jnp.mean(values_f, axis=-1, keepdims=True)
    centred = values_f - mean_value
    variance = jnp.mean(centred * centred, axis=-1, keepdims=True)
    return (centred * lax.rsqrt(variance + 1e-05) * gain).astype(jnp.bfloat16)


def dot(left, right):
    return jnp.dot(left, right, preferred_element_type=jnp.float32)


def fill_bias(rel_ref, rows_ref, full_ref, q_rows, k_rows, row_off, k_cols, col_places, first_key, groups):
    heads, entries = rel_ref.shape
    classes = math.isqrt(entries)
    q_cols = rows_ref.shape[1] // heads
    extent = q_rows + k_rows - 1
    before = q_rows - 1 + row_off - REACH
    chunks = -(-extent * k_cols // 128)
    width = chunks * 128
    place = lax.broadcasted_iota(jnp.int32, (1, width), 1)
    entry = lax.broadcasted_iota(jnp.int32, (entries, 1), 0)
    across = place // k_cols
    key_col = col_places(place - across * k_cols)
    down = across - before
    table = rel_ref[...] * LOG2E
    for j in range(q_cols):
        over = key_col - j + REACH
        known = (down >= 0) & (down < classes) & (over >= 0) & (over < classes)
        target = jnp.where(known, down * classes + over, -1)
        hot = (entry == target).astype(jnp.float32)
        found = jnp.dot(
            table, hot, precision=lax.Precision.HIGHEST, preferred_element_type=jnp.float32
        )
        for c in range(chunks):
            rows_ref[c, j * heads : (j + 1) * heads, :] = found[:, c * 128 : (c + 1) * 128]
    n_key = k_rows * k_cols
    for n in range(heads):
        strips = jnp.concatenate(
            [rows_ref[c, pl.ds(n, q_cols, stride=heads), :] for c in range(chunks)], axis=1
        )
        for i in range(q_rows):
            start = (q_rows - 1 - i) * k_cols
            strip = jnp.concatenate([strips[:, start : start + n_key]] * groups, axis=1)
            for t in range(groups):
                first = t * n_key + i * q_cols
                full_ref[n, first : first + q_cols, first_key : first_key + groups * n_key] = strip


def slot_places(index, shape):
    tile_cols, residue_rows, residue_cols, block_rows, block_cols, col_count, slot = shape
    row = index // tile_cols
    col = index - row * tile_cols
    row_block = row // DILATION
    col_block = col // DILATION
    row, col = row - row_block * DILATION, col - col_block * DILATION
    peer_row = row // residue_rows
    peer_col = col // residue_cols
    inner = (row - peer_row * residue_rows) * residue_cols + col - peer_col * residue_cols
    inner = (inner * block_rows + row_block) * block_cols + col_block
    return (peer_row * col_count + peer_col) * slot + inner


def group_places(index, shape):
    _, residue_rows, residue_cols, block_rows, block_cols, col_count, slot, row_count = shape
    used = residue_rows * residue_cols * block_rows * block_cols
    peer = index // slot
    inner = index - peer * slot
    peer_row = peer // col_count
    peer_col = peer - peer_row * col_count
    rest = inner // block_cols
    col_block = inner - rest * block_cols
    residue = rest // block_rows
    row_block = rest - residue * block_rows
    place = residue * (block_rows * row_count) + peer_row * block_rows + row_block
    place = place * (block_cols * col_count) + peer_col * block_cols + col_block
    return jnp.where(inner < used, place, -1)


def column(count):
    return lax.broadcasted_iota(jnp.int32, (count, 1), 0)


def line(count):
    return lax.broadcasted_iota(jnp.int32, (1, count), 1)


def one_hot(left, right):
    return jnp.where(left == right, 1.0, 0.0).astype(jnp.bfloat16)


def in_window(query, key, extent):
    start = jnp.clip(query - 3, 0, extent - 7)
    return (key >= start) & (key < start + 7)


def head_lanes(lanes, head_size):
    lane = lax.broadcasted_iota(jnp.int32, (1, lanes), 1)
    return [(lane // head_size) == h for h in range(lanes // head_size)]


def attend(queries, keys, values, bias, mask, head_size):
    count, lanes = queries.shape
    picks = head_lanes(lanes, head_size)
    zero = jnp.zeros_like(queries)
    stacked = jnp.concatenate([jnp.where(pick, queries, zero) for pick in picks], axis=0)
    scores = lax.dot_general(
        stacked, keys, (((1,), (1,)), ((), ())), preferred_element_type=jnp.float32
    )
    scores = scores.reshape(len(picks), count, keys.shape[0]) + bias
    if mask is not None:
        scores = scores + mask[None]
    peak = jnp.max(scores, axis=-1, keepdims=True)
    weights = jnp.exp2(scores - peak).astype(jnp.bfloat16)
    wide = jnp.concatenate([values, jnp.ones_like(values)], axis=1)
    summed = dot(weights.reshape(len(picks) * count, keys.shape[0]), wide)
    ratio = summed[:, :lanes] / summed[:, lanes:]
    result = ratio[:count]
    for h in range(1, len(picks)):
        result = jnp.where(picks[h], ratio[h * count : (h + 1) * count], result)
    return result.astype(jnp.bfloat16)


def finish(attended, stream, gain, proj_ref, up_ref, down_ref):
    hidden_width = up_ref.shape[1]
    part = math.gcd(hidden_width, 512)
    mixed = (dot(attended, proj_ref[...]) + stream.astype(jnp.float32)).astype(jnp.bfloat16)
    normed = layer_norm(mixed, gain)
    total = mixed.astype(jnp.float32)
    for first in range(0, hidden_width, part):
        hidden = jax.nn.gelu(dot(normed, up_ref[:, first : first + part]), approximate=True)
        total = total + dot(hidden.astype(jnp.bfloat16), down_ref[first : first + part, :])
    return total.astype(jnp.bfloat16)


def project(src_ref, gain, weight, dst_ref, scale, spans):
    for first, last in spans:
        result = dot(layer_norm(src_ref[first:last, :], gain), weight)
        if scale is not None:
            result = result * scale
        dst_ref[first:last, :] = result.astype(jnp.bfloat16)


def both_layers(
    geometry, x_ref, gains_ref, rel_ref, qkv_hbm, proj_hbm, up_hbm, down_hbm, out_ref,
    qkv_all, proj_all, up_all, down_all, q_ref, kv_ref, pad_ref, edge_ref, full_ref, full_two_ref,
    bias_ref, bias_two_ref, att_ref, att_two_ref, send_ref, arrive_ref, x_two_ref, reply_ref, back_ref,
    weight_sem, halo_send, halo_recv, go_send, go_recv, back_send, back_recv,
):
    row_count, col_count, tile_rows, tile_cols, heads, pack, places = geometry
    _, residue_rows, residue_cols, block_rows, block_cols, _, slot, _ = places
    tokens, width = x_ref.shape
    peers = row_count * col_count
    map_rows, map_cols = tile_rows * row_count, tile_cols * col_count
    group_rows, group_cols = block_rows * row_count, block_cols * col_count
    head_size = width // heads
    lanes = 128
    per = lanes // head_size
    scale = head_size ** (-0.5) * LOG2E
    my_row, my_col = lax.axis_index("row"), lax.axis_index("col")
    me = my_row * col_count + my_col

    def weight_copy(index, layer):
        src, dst = (
            (qkv_hbm, qkv_all), (proj_hbm, proj_all), (up_hbm, up_all), (down_hbm, down_all)
        )[index]
        return pltpu.make_async_copy(src.at[layer], dst.at[layer], weight_sem.at[index, layer])

    for layer in range(2):
        for index in range(4):
            weight_copy(index, layer).start()

    rim = HALO * tile_cols
    side = (tile_rows + 2 * HALO) * HALO
    own = tokens + 2 * rim
    corner = HALO * HALO
    edge = tile_rows * HALO
    pad_ref[0:rim, :] = jnp.zeros((rim, width), jnp.bfloat16)
    pad_ref[rim + tokens :, :] = jnp.zeros((rim + 2 * side, width), jnp.bfloat16)
    place = column(edge)
    source = place // HALO * tile_cols + place - place // HALO * HALO
    edge_ref[0:edge, :] = dot(one_hot(source, line(tokens)), x_ref[...]).astype(jnp.bfloat16)
    edge_ref[edge : 2 * edge, :] = dot(
        one_hot(source + tile_cols - HALO, line(tokens)), x_ref[...]
    ).astype(jnp.bfloat16)

    barrier = pltpu.get_barrier_semaphore()

    def greet(peer, carry):
        @pl.when(peer != me)
        def _():
            pl.semaphore_signal(
                barrier,
                inc=1,
                device_id=(peer // col_count, peer % col_count),
                device_id_type=pl.DeviceIdType.MESH,
            )

        return carry

    lax.fori_loop(0, peers, greet, 0)
    pl.semaphore_wait(barrier, peers - 1)

    left, right = own, own + side
    moves = (
        (-1, 0, x_ref, 0, rim + tokens, rim),
        (1, 0, x_ref, tokens - rim, 0, rim),
        (0, 1, edge_ref, edge, left + corner, edge),
        (0, -1, edge_ref, 0, right + corner, edge),
        (-1, 1, edge_ref, edge, left + corner + edge, corner),
        (-1, -1, edge_ref, 0, right + corner + edge, corner),
        (1, 1, edge_ref, 2 * edge - corner, left, corner),
        (1, -1, edge_ref, edge - corner, right, corner),
    )

    def exists(down, over):
        row, col = my_row + down, my_col + over
        return (row >= 0) & (row < row_count) & (col >= 0) & (col < col_count)

    def halo_copy(k):
        down, over, src, first, there, rows = moves[k]
        return pltpu.make_async_remote_copy(
            src_ref=src.at[first : first + rows],
            dst_ref=pad_ref.at[there : there + rows],
            send_sem=halo_send.at[k],
            recv_sem=halo_recv.at[k],
            device_id=(my_row + down, my_col + over),
            device_id_type=pl.DeviceIdType.MESH,
        )

    for k in range(len(moves)):

        @pl.when(exists(moves[k][0], moves[k][1]))
        def _(k=k):
            halo_copy(k).start()

    pad_ref[rim : rim + tokens, :] = x_ref[...]
    key_rows = QUERY_ROWS + 2 * HALO
    n_query = QUERY_ROWS * tile_cols
    sets = (
        (0, tile_cols, 0, lambda col: col),
        (own, HALO, key_rows * tile_cols, lambda col: col - HALO),
        (own + side, HALO, key_rows * (tile_cols + HALO), lambda col: col + tile_cols),
    )
    for _, k_cols, first_key, col_places in sets:
        fill_bias(
            rel_ref.at[0], bias_ref, full_ref, QUERY_ROWS, key_rows, HALO, k_cols, col_places,
            first_key, 1,
        )
    gain = gains_ref[0:1, :]
    weight_copy(0, 0).wait()
    project(x_ref, gain, qkv_all[0, :, :width], q_ref, scale, ((0, tokens),))
    kv_weight = qkv_all[0, :, width:]
    project(pad_ref, gain, kv_weight, kv_ref, None, ((rim, rim + tokens),))
    for k in range(len(moves)):

        @pl.when(exists(-moves[k][0], -moves[k][1]))
        def _(k=k):
            halo_copy(k).wait_recv()

    project(pad_ref, gain, kv_weight, kv_ref, None, ((0, rim), (rim + tokens, own + 2 * side)))

    first_row = my_row * tile_rows
    first_col = my_col * tile_cols
    query = column(n_query)
    query_row = query // tile_cols
    query_col = first_col + query - query_row * tile_cols
    seen_cols, key_row_list = [], []
    for _, k_cols, _, col_places in sets:
        key = line(key_rows * k_cols)
        key_row = key // k_cols
        key_row_list.append(key_row)
        key_col = first_col + col_places(key - key_row * k_cols)
        seen_cols.append(in_window(query_col, key_col, map_cols))
    for index in range(1, 4):
        weight_copy(index, 0).wait()

    def slot_rows(peer):
        return pl.ds(pl.multiple_of(peer * slot, slot), slot)

    def exchange(src, dst, send, recv, peer):
        return pltpu.make_async_remote_copy(
            src_ref=src.at[slot_rows(peer)],
            dst_ref=dst.at[slot_rows(me)],
            send_sem=send.at[peer],
            recv_sem=recv.at[me],
            device_id=(peer // col_count, peer % col_count),
            device_id_type=pl.DeviceIdType.MESH,
        )

    def send_slots(src, dst, send, recv, first, count):
        def one(p, carry):
            peer = first + (me + p) % count

            @pl.when(peer != me)
            def _():
                exchange(src, dst, send, recv, peer).start()

            @pl.when(peer == me)
            def _():
                dst[slot_rows(me), :] = src[slot_rows(me), :]

            return carry

        lax.fori_loop(0, count, one, 0)

    def wait_slots(src, dst, send, recv, sent):
        def one(peer, carry):
            @pl.when(peer != me)
            def _():
                if sent:
                    exchange(src, dst, send, recv, peer).wait_send()
                else:
                    pltpu.make_async_remote_copy(
                        src_ref=src.at[slot_rows(peer)],
                        dst_ref=dst.at[slot_rows(peer)],
                        send_sem=send.at[peer],
                        recv_sem=recv.at[peer],
                        device_id=(peer // col_count, peer % col_count),
                        device_id_type=pl.DeviceIdType.MESH,
                    ).wait_recv()

            return carry

        lax.fori_loop(0, peers, one, 0)

    halves = DILATION // QUERY_ROWS
    half_peers = peers // halves
    half_slots = half_peers * slot

    def half(h, carry):
        def step(k, inner):
            block = h + halves * k
            top = first_row + block * QUERY_ROWS
            masks = [
                jnp.where(
                    col_seen & in_window(top + query_row, top + key_row - HALO, map_rows), 0.0, MASKED
                )
                for col_seen, key_row in zip(seen_cols, key_row_list)
            ]
            mask = jnp.concatenate(masks, axis=1).astype(jnp.float32)
            q_rows = pl.ds(pl.multiple_of(block * n_query, n_query), n_query)
            to_rows = pl.ds(pl.multiple_of(k * n_query, n_query), n_query)
            k_rows = []
            for base, k_cols, _, _ in sets:
                stride = QUERY_ROWS * k_cols
                k_rows.append(pl.ds(pl.multiple_of(base + block * stride, 16), key_rows * k_cols))
            for g in range(width // lanes):
                cols = slice(g * lanes, (g + 1) * lanes)
                v_cols = slice(width + g * lanes, width + (g + 1) * lanes)
                att_ref[to_rows, cols] = attend(
                    q_ref[q_rows, cols],
                    jnp.concatenate([kv_ref[rows, cols] for rows in k_rows], axis=0),
                    jnp.concatenate([kv_ref[rows, v_cols] for rows in k_rows], axis=0),
                    full_ref[g * per : (g + 1) * per],
                    mask,
                    head_size,
                )
            return inner

        lax.fori_loop(0, block_rows, step, 0)
        blocks = [h + halves * k for k in range(block_rows)]
        stream = jnp.concatenate(
            [x_ref[pl.ds(pl.multiple_of(at * n_query, n_query), n_query), :] for at in blocks], axis=0
        )
        result = finish(
            att_ref[...], stream, gains_ref[1:2, :], proj_all.at[0], up_all.at[0], down_all.at[0]
        )
        here = line(block_rows * n_query)
        which = here // n_query
        token = (h + halves * which) * n_query + here - which * n_query
        hot = one_hot(h * half_slots + column(half_slots), slot_places(token, places[:7]))
        rows = pl.ds(pl.multiple_of(h * half_slots, half_slots), half_slots)
        send_ref[rows, :] = dot(hot, result).astype(jnp.bfloat16)
        send_slots(send_ref, arrive_ref, go_send, go_recv, h * half_peers, half_peers)
        return carry

    lax.fori_loop(0, halves, half, 0)

    size = group_rows * group_cols
    n_two = pack * size
    query, key = column(n_two), line(n_two)
    query_row, key_row = query // group_cols, key // group_cols
    query_col, key_col = query - query_row * group_cols, key - key_row * group_cols
    query_group, key_group = query // size, key // size
    seen = (
        (query_group == key_group)
        & in_window(query_row - query_group * group_rows, key_row - key_group * group_rows, group_rows)
        & in_window(query_col, key_col, group_cols)
    )
    fill_bias(
        rel_ref.at[1], bias_two_ref, full_two_ref, group_rows, group_rows, 0, group_cols,
        lambda col: col, 0, pack,
    )
    for n in range(heads):
        full_two_ref[n] = jnp.where(seen, full_two_ref[n], MASKED)
    for index in range(4):
        weight_copy(index, 1).wait()
    arrivals = peers * slot
    hot = one_hot(column(tokens), group_places(line(arrivals), places))
    wait_slots(send_ref, arrive_ref, go_send, go_recv, False)

    x_two_ref[...] = dot(hot, arrive_ref[...]).astype(jnp.bfloat16)
    gain = gains_ref[2:3, :]
    project(x_two_ref, gain, qkv_all[1, :, :width], q_ref, scale, ((0, tokens),))
    project(x_two_ref, gain, qkv_all[1, :, width:], kv_ref, None, ((0, tokens),))

    def step_two(block, carry):
        rows = pl.ds(pl.multiple_of(block * n_two, n_two), n_two)
        for g in range(width // lanes):
            cols = slice(g * lanes, (g + 1) * lanes)
            v_cols = slice(width + g * lanes, width + (g + 1) * lanes)
            att_two_ref[rows, cols] = attend(
                q_ref[rows, cols],
                kv_ref[rows, cols],
                kv_ref[rows, v_cols],
                full_two_ref[g * per : (g + 1) * per],
                None,
                head_size,
            )
        return carry

    lax.fori_loop(0, tokens // n_two, step_two, 0)

    def half_two(h, carry):
        rows = pl.ds(pl.multiple_of(h * half_slots, half_slots), half_slots)
        spots = group_places(h * half_slots + column(half_slots), places)
        attended = dot(one_hot(spots, line(tokens)), att_two_ref[...]).astype(jnp.bfloat16)
        reply_ref[rows, :] = finish(
            attended, arrive_ref[rows, :], gains_ref[3:4, :], proj_all.at[1], up_all.at[1], down_all.at[1]
        )
        send_slots(reply_ref, back_ref, back_send, back_recv, h * half_peers, half_peers)
        return carry

    lax.fori_loop(0, halves, half_two, 0)
    wait_slots(send_ref, arrive_ref, go_send, go_recv, True)
    for k in range(len(moves)):

        @pl.when(exists(moves[k][0], moves[k][1]))
        def _(k=k):
            halo_copy(k).wait_send()

    hot = one_hot(slot_places(column(tokens), places[:7]), line(arrivals))
    wait_slots(reply_ref, back_ref, back_send, back_recv, False)
    out_ref[...] = dot(hot, back_ref[...]).astype(jnp.bfloat16)
    wait_slots(reply_ref, back_ref, back_send, back_recv, True)


def body(tokens, norm_gains, qkv_weight, rel_bias, proj_weight, up_weight, down_weight):
    tile_rows, tile_cols, width = tokens.shape
    row_count = lax.axis_size("row")
    col_count = lax.axis_size("col")
    heads = rel_bias.shape[1]
    rel = rel_bias.reshape(rel_bias.shape[0], heads, -1)
    residue_rows = DILATION // row_count
    residue_cols = DILATION // col_count
    block_rows = tile_rows // DILATION
    block_cols = tile_cols // DILATION
    group_rows = block_rows * row_count
    group_cols = block_cols * col_count
    size = group_rows * group_cols
    pack = max(1, 128 // size)
    peers = row_count * col_count
    count = tile_rows * tile_cols
    slot = -(-(count // peers) // 16) * 16
    places = (
        tile_cols, residue_rows, residue_cols, block_rows, block_cols, col_count, slot, row_count
    )
    geometry = (row_count, col_count, tile_rows, tile_cols, heads, pack, places)
    key_rows = QUERY_ROWS + 2 * HALO
    n_query = QUERY_ROWS * tile_cols
    n_key = key_rows * (tile_cols + 2 * HALO)
    padded = count + 2 * HALO * tile_cols + 2 * HALO * (tile_rows + 2 * HALO)
    chunks = -(-(QUERY_ROWS + key_rows - 1) * tile_cols // 128)
    chunks_two = -(-(2 * group_rows - 1) * group_cols // 128)
    slots = peers * slot
    half = jnp.bfloat16
    weights = (qkv_weight, proj_weight, up_weight, down_weight)
    vmem = pl.BlockSpec(memory_space=pltpu.VMEM)
    hbm = pl.BlockSpec(memory_space=pl.ANY)
    result = pl.pallas_call(
        functools.partial(both_layers, geometry),
        out_shape=jax.ShapeDtypeStruct((count, width), half),
        in_specs=[vmem, vmem, vmem, hbm, hbm, hbm, hbm],
        out_specs=vmem,
        scratch_shapes=[pltpu.VMEM(weight.shape, weight.dtype) for weight in weights]
        + [
            pltpu.VMEM((count, width), half),
            pltpu.VMEM((padded, 2 * width), half),
            pltpu.VMEM((padded, width), half),
            pltpu.VMEM((2 * tile_rows * HALO, width), half),
            pltpu.VMEM((heads, n_query, n_key), jnp.float32),
            pltpu.VMEM((heads, pack * size, pack * size), jnp.float32),
            pltpu.VMEM((chunks, tile_cols * heads, 128), jnp.float32),
            pltpu.VMEM((chunks_two, group_cols * heads, 128), jnp.float32),
            pltpu.VMEM((block_rows * n_query, width), half),
            pltpu.VMEM((count, width), half),
            pltpu.VMEM((slots, width), half),
            pltpu.VMEM((slots, width), half),
            pltpu.VMEM((count, width), half),
            pltpu.VMEM((slots, width), half),
            pltpu.VMEM((slots, width), half),
            pltpu.SemaphoreType.DMA((4, 2)),
            pltpu.SemaphoreType.DMA((8,)),
            pltpu.SemaphoreType.DMA((8,)),
            pltpu.SemaphoreType.DMA((peers,)),
            pltpu.SemaphoreType.DMA((peers,)),
            pltpu.SemaphoreType.DMA((peers,)),
            pltpu.SemaphoreType.DMA((peers,)),
        ],
        compiler_params=pltpu.CompilerParams(
            collective_id=0, has_side_effects=True, vmem_limit_bytes=VMEM_BYTES
        ),
    )(tokens.reshape(count, width), norm_gains, rel, *weights)
    return result.reshape(tile_rows, tile_cols, width)


def solution(mesh):
    placed = (P("row", "col", None), P(), P(), P(), P(), P(), P())
    return jax.shard_map(
        body, mesh=mesh, in_specs=placed, out_specs=P("row", "col", None), check_vma=False
    )
```

time: 107 us -> 70.3 us (0.66)
  blocking collectives: 44.5 us -> 0 us
  Pallas kernels: 44.9 us -> 66.6 us
  starting transfers between devices: 9.44 us -> 0 us
  waiting for transfers between devices: 2.51 us -> 0 us
  local copies, waits for them, and re-layouts: 5.08 us -> 3.51 us
    all_to_all x2 -> x0, blocking collectives: 44.5 us -> none  [body(): lax.all_to_all(sent.reshape(peers, slot, width), ('row', 'col'), split_ax...]
    pallas_call x3 -> x1, Pallas kernels: 44.9 us -> 66.6 us  [body(): pl.pallas_call(functools.partial(both_layers, geometry), out_shape=jax.Sh...]
    ppermute x4 -> x0, starting transfers between devices: 9.44 us -> none  [the longest x2 6.86 us: from_both(): lax.ppermute(tail, axis, [(i, i + 1) for i in range(count - 1)])]
    ppermute x4 -> x0, waiting for transfers between devices: 2.51 us -> none  [the longest x2 1.81 us: from_both(): lax.ppermute(head, axis, [(i + 1, i) for i in range(count - 1)])]
    slice x4 -> x0, local copies, waits for them, and re-layouts: 2.05 us -> none  [the longest x1 1.14 us: body(): tokens[:, :HALO]]
    unnamed x4 -> x1, local copies, waits for them, and re-layouts: 0.01 us -> 1.87 us
    reshape x2 -> x0, local copies, waits for them, and re-layouts: 1.39 us -> none  [body(): piece.reshape(-1, width)]
  transfers between devices with their start and end apart: 4 -> 0, of which waited for: 2 -> 0; matrix products, arithmetic and copies ran while one was open for 3% -> 0% of each run, Pallas kernels for 0% -> 0%
where the time goes in v3:
time: 70.3 us; the launch traced here: 70.1 us
  Pallas kernels  66.6 us (95%)
  local copies, waits for them, and re-layouts  3.51 us (5%)
    pallas_call x1, Pallas kernels, body(): pl.pallas_call(functools.partial(both_layers, geometry), out_shape=jax.Sh...  66.6 us
    unnamed x1, local copies, waits for them, and re-layouts  1.87 us
    reshape x1, local copies, waits for them, and re-layouts, body(): rel = rel_bias.reshape(rel_bias.shape[0], heads, -1)  1.64 us

profile of v3, /device:TPU:0, one launch (start us, length us, event | category | flops | bytes accessed | tf_op | source)
XLA Modules:
  0.0 70.1 jit_solution(13351641361765843429)
XLA Ops:
  0.0 1.6 %copy.10.rel_ref = f32[2,16,169]{2,1,0:T(8,128)} copy(f32[2,16,169]{1,0,2:T(2,128)} %bitcast.5) | data formatting | bytes 43264 | tf_op jit(solution)/shard_map/reshape | solution.py:473
  1.6 66.6 %shard_map.73 = bf16[512,512]{1,0:T(8,128)(2,1)} custom-call(bf16[512,512]{1,0:T(8,128)(2,1)} %bitcast.4, f32[4,512]{1,0:T(4,128)} %gains_ref.1, f32[2,16,169]{2,1,0:T(8,128)} %copy.10.rel_ref, bf16[2,512,1536]{2,1,0:T(8,128)(2,1)} %qkv_hbm.1, bf16[2,512,512]{2,1,0:T(8,128)(2,1)} %proj_hbm.1, bf16[2,512,2048]{2,1,0:T(8,128)(2,1)} %up_hbm.1, ...), custom_call_target="tpu_custom_call" | custom-call | tf_op jit(solution)/shard_map/pallas_call | solution.py:500
  68.2 1.9 %copy.12 = bf16[32,16,512]{2,1,0:T(8,128)(2,1)} copy(bf16[32,16,512]{2,1,0:T(8,128)(2,1)} %bitcast.3) | data formatting | bytes 1048576

commit v4 on v3

--- a/solution.py
+++ b/solution.py
@@ -30,8 +30,8 @@
 
 
 def fill_bias(rel_ref, rows_ref, full_ref, q_rows, k_rows, row_off, k_cols, col_places, first_key, groups):
-    heads, entries = rel_ref.shape
-    classes = math.isqrt(entries)
+    heads, classes, _ = rel_ref.shape
+    entries = classes * classes
     q_cols = rows_ref.shape[1] // heads
     extent = q_rows + k_rows - 1
     before = q_rows - 1 + row_off - REACH
@@ -42,15 +42,18 @@
     across = place // k_cols
     key_col = col_places(place - across * k_cols)
     down = across - before
-    table = rel_ref[...] * LOG2E
+    table = jnp.concatenate([rel_ref[:, dy, :] for dy in range(classes)], axis=1) * LOG2E
+    parts = []
+    for _ in range(3):
+        parts.append(table.astype(jnp.bfloat16))
+        table = table - parts[-1].astype(jnp.float32)
+    stacked = jnp.concatenate(parts, axis=0)
     for j in range(q_cols):
         over = key_col - j + REACH
         known = (down >= 0) & (down < classes) & (over >= 0) & (over < classes)
         target = jnp.where(known, down * classes + over, -1)
-        hot = (entry == target).astype(jnp.float32)
-        found = jnp.dot(
-            table, hot, precision=lax.Precision.HIGHEST, preferred_element_type=jnp.float32
-        )
+        found = dot(stacked, one_hot(entry, target))
+        found = found[:heads] + found[heads : 2 * heads] + found[2 * heads :]
         for c in range(chunks):
             rows_ref[c, j * heads : (j + 1) * heads, :] = found[:, c * 128 : (c + 1) * 128]
     n_key = k_rows * k_cols
@@ -347,7 +350,9 @@
     half_peers = peers // halves
     half_slots = half_peers * slot
 
-    def half(h, carry):
+    def half(turn, carry):
+        h = (turn + my_col) % halves
+
         def step(k, inner):
             block = h + halves * k
             top = first_row + block * QUERY_ROWS
@@ -441,7 +446,8 @@
 
     lax.fori_loop(0, tokens // n_two, step_two, 0)
 
-    def half_two(h, carry):
+    def half_two(turn, carry):
+        h = (turn + my_col) % halves
         rows = pl.ds(pl.multiple_of(h * half_slots, half_slots), half_slots)
         spots = group_places(h * half_slots + column(half_slots), places)
         attended = dot(one_hot(spots, line(tokens)), att_two_ref[...]).astype(jnp.bfloat16)
@@ -470,7 +476,6 @@
     row_count = lax.axis_size("row")
     col_count = lax.axis_size("col")
     heads = rel_bias.shape[1]
-    rel = rel_bias.reshape(rel_bias.shape[0], heads, -1)
     residue_rows = DILATION // row_count
     residue_cols = DILATION // col_count
     block_rows = tile_rows // DILATION
@@ -530,7 +535,7 @@
         compiler_params=pltpu.CompilerParams(
             collective_id=0, has_side_effects=True, vmem_limit_bytes=VMEM_BYTES
         ),
-    )(tokens.reshape(count, width), norm_gains, rel, *weights)
+    )(tokens.reshape(count, width), norm_gains, rel_bias, *weights)
     return result.reshape(tile_rows, tile_cols, width)
 
 

time: 70.3 us -> 64.3 us (0.915)
  Pallas kernels: 66.6 us -> 60.4 us
    pallas_call x1, Pallas kernels: 66.6 us -> 60.4 us  [body(): pl.pallas_call(functools.partial(both_layers, geometry), out_shape=jax.Sh...]
    unnamed x1 -> x2, local copies, waits for them, and re-layouts: 1.87 us -> 3.71 us
    reshape x1 -> x0, local copies, waits for them, and re-layouts: 1.64 us -> none  [body(): rel = rel_bias.reshape(rel_bias.shape[0], heads, -1)]
where the time goes in v4:
time: 64.3 us; the launch traced here: 64.1 us
  Pallas kernels  60.4 us (94%)
  local copies, waits for them, and re-layouts  3.71 us (6%)
    pallas_call x1, Pallas kernels, body(): pl.pallas_call(functools.partial(both_layers, geometry), out_shape=jax.Sh...  60.4 us
    unnamed x2, local copies, waits for them, and re-layouts  3.71 us

profile of v4, /device:TPU:0, one launch (start us, length us, event | category | flops | bytes accessed | tf_op | source)
XLA Modules:
  0.0 64.1 jit_solution(4607207741935322930)
XLA Ops:
  0.0 1.8 %copy.8.rel_ref = f32[2,16,13,13]{3,2,1,0:T(8,128)} copy(f32[2,16,13,13]{1,0,3,2:T(2,128)} %param.10) | data formatting | bytes 43264 | tf_op args[3]
  1.8 60.4 %shard_map.73 = bf16[512,512]{1,0:T(8,128)(2,1)} custom-call(bf16[512,512]{1,0:T(8,128)(2,1)} %bitcast.3, f32[4,512]{1,0:T(4,128)} %gains_ref.1, f32[2,16,13,13]{3,2,1,0:T(8,128)} %copy.8.rel_ref, bf16[2,512,1536]{2,1,0:T(8,128)(2,1)} %qkv_hbm.1, bf16[2,512,512]{2,1,0:T(8,128)(2,1)} %proj_hbm.1, bf16[2,512,2048]{2,1,0:T(8,128)(2,1)} %up_hbm.1, ...), custom_call_target="tpu_custom_call" | custom-call | tf_op jit(solution)/shard_map/pallas_call | solution.py:505
  62.3 1.9 %copy.10 = bf16[32,16,512]{2,1,0:T(8,128)(2,1)} copy(bf16[32,16,512]{2,1,0:T(8,128)(2,1)} %bitcast.2) | data formatting | bytes 1048576

commit v5 on v4

--- a/solution.py
+++ b/solution.py
@@ -30,7 +30,7 @@
 
 
 def fill_bias(rel_ref, rows_ref, full_ref, q_rows, k_rows, row_off, k_cols, col_places, first_key, groups):
-    heads, classes, _ = rel_ref.shape
+    classes, _, heads = rel_ref.shape
     entries = classes * classes
     q_cols = rows_ref.shape[1] // heads
     extent = q_rows + k_rows - 1
@@ -42,12 +42,12 @@
     across = place // k_cols
     key_col = col_places(place - across * k_cols)
     down = across - before
-    table = jnp.concatenate([rel_ref[:, dy, :] for dy in range(classes)], axis=1) * LOG2E
+    table = jnp.concatenate([rel_ref[dy] for dy in range(classes)], axis=0) * LOG2E
     parts = []
     for _ in range(3):
         parts.append(table.astype(jnp.bfloat16))
         table = table - parts[-1].astype(jnp.float32)
-    stacked = jnp.concatenate(parts, axis=0)
+    stacked = jnp.concatenate([part.T for part in parts], axis=0)
     for j in range(q_cols):
         over = key_col - j + REACH
         known = (down >= 0) & (down < classes) & (over >= 0) & (over < classes)
@@ -221,6 +221,16 @@
         return carry
 
     lax.fori_loop(0, peers, greet, 0)
+    key_rows = QUERY_ROWS + 2 * HALO
+    n_query = QUERY_ROWS * tile_cols
+    sets = (
+        (0, tile_cols, 0, lambda col: col),
+        (own, HALO, key_rows * tile_cols, lambda col: col - HALO),
+        (own + side, HALO, key_rows * (tile_cols + HALO), lambda col: col + tile_cols),
+    )
+    fill_bias(
+        rel_ref.at[:, :, 0], bias_ref, full_ref, QUERY_ROWS, key_rows, HALO, tile_cols, sets[0][3], 0, 1
+    )
     pl.semaphore_wait(barrier, peers - 1)
 
     left, right = own, own + side
@@ -257,16 +267,9 @@
             halo_copy(k).start()
 
     pad_ref[rim : rim + tokens, :] = x_ref[...]
-    key_rows = QUERY_ROWS + 2 * HALO
-    n_query = QUERY_ROWS * tile_cols
-    sets = (
-        (0, tile_cols, 0, lambda col: col),
-        (own, HALO, key_rows * tile_cols, lambda col: col - HALO),
-        (own + side, HALO, key_rows * (tile_cols + HALO), lambda col: col + tile_cols),
-    )
-    for _, k_cols, first_key, col_places in sets:
+    for _, k_cols, first_key, col_places in sets[1:]:
         fill_bias(
-            rel_ref.at[0], bias_ref, full_ref, QUERY_ROWS, key_rows, HALO, k_cols, col_places,
+            rel_ref.at[:, :, 0], bias_ref, full_ref, QUERY_ROWS, key_rows, HALO, k_cols, col_places,
             first_key, 1,
         )
     gain = gains_ref[0:1, :]
@@ -413,7 +416,7 @@
         & in_window(query_col, key_col, group_cols)
     )
     fill_bias(
-        rel_ref.at[1], bias_two_ref, full_two_ref, group_rows, group_rows, 0, group_cols,
+        rel_ref.at[:, :, 1], bias_two_ref, full_two_ref, group_rows, group_rows, 0, group_cols,
         lambda col: col, 0, pack,
     )
     for n in range(heads):
@@ -535,7 +538,7 @@
         compiler_params=pltpu.CompilerParams(
             collective_id=0, has_side_effects=True, vmem_limit_bytes=VMEM_BYTES
         ),
-    )(tokens.reshape(count, width), norm_gains, rel_bias, *weights)
+    )(tokens.reshape(count, width), norm_gains, rel_bias.transpose(2, 3, 0, 1), *weights)
     return result.reshape(tile_rows, tile_cols, width)
 
 

time: 64.3 us -> 62.3 us (0.969)
  local copies, waits for them, and re-layouts: 3.71 us -> 1.87 us
    unnamed x2 -> x1, local copies, waits for them, and re-layouts: 3.71 us -> 1.87 us
where the time goes in v5:
time: 62.3 us; the launch traced here: 62.2 us
  Pallas kernels  60.3 us (97%)
  local copies, waits for them, and re-layouts  1.87 us (3%)
    pallas_call x1, Pallas kernels, body(): pl.pallas_call(functools.partial(both_layers, geometry), out_shape=jax.Sh...  60.3 us
    unnamed x1, local copies, waits for them, and re-layouts  1.87 us

profile of v5, /device:TPU:0, one launch (start us, length us, event | category | flops | bytes accessed | tf_op | source)
XLA Modules:
  0.0 62.2 jit_solution(756952474462590017)
XLA Ops:
  0.0 60.3 %shard_map.73 = bf16[512,512]{1,0:T(8,128)(2,1)} custom-call(bf16[512,512]{1,0:T(8,128)(2,1)} %bitcast.4, f32[4,512]{1,0:T(4,128)} %gains_ref.1, f32[13,13,2,16]{3,2,1,0:T(2,128)} %bitcast.5, bf16[2,512,1536]{2,1,0:T(8,128)(2,1)} %qkv_hbm.1, bf16[2,512,512]{2,1,0:T(8,128)(2,1)} %proj_hbm.1, bf16[2,512,2048]{2,1,0:T(8,128)(2,1)} %up_hbm.1, ...), custom_call_target="tpu_custom_call" | custom-call | tf_op jit(solution)/shard_map/pallas_call | solution.py:508
  60.3 1.9 %copy.9 = bf16[32,16,512]{2,1,0:T(8,128)(2,1)} copy(bf16[32,16,512]{2,1,0:T(8,128)(2,1)} %bitcast.3) | data formatting | bytes 1048576
